TPU v7x, 32 devices: a whole 2x2x4 slice. The times are simulated.
32 devices in a mesh: grp: 2 (over x), samp: 16 (over z, y, core).
Axes of the slice: x: 2, y: 2, z: 4, core: 2. Of those that a mesh axis runs over, the one named last changes fastest.
Arguments:
- tokens: bfloat16 [2, 1536, 8, 512], P('grp', 'samp'), may hold values from -6 to 6
- segments: int32 [2, 1536], P('grp', 'samp'), may hold values from -1 to 3, as said below
- cotangent: bfloat16 [2, 1536, 8, 512], P('grp', 'samp'), may hold values from -6 to 6
- first_gain: float32 [512], replicated, may hold values from 0.1 to 1.9
- first_shift: float32 [512], replicated, may hold values from -3 to 3
- sample_qkv: bfloat16 [512, 1536], replicated, may hold values from -0.25 to 0.25
- sample_out: bfloat16 [512, 512], replicated, may hold values from -0.75 to 0.75
- second_gain: float32 [512], replicated, may hold values from 0.1 to 1.9
- second_shift: float32 [512], replicated, may hold values from -3 to 3
- feature_qkv: bfloat16 [512, 1536], replicated, may hold values from -0.25 to 0.25
- feature_out: bfloat16 [512, 512], replicated, may hold values from -0.75 to 0.75
- third_gain: float32 [512], replicated, may hold values from 0.1 to 1.9
- third_shift: float32 [512], replicated, may hold values from -3 to 3
- up_weight: bfloat16 [512, 2048], replicated, may hold values from -0.25 to 0.25
- up_bias: float32 [2048], replicated, may hold values from -3 to 3
- down_weight: bfloat16 [2048, 512], replicated, may hold values from -0.125 to 0.125
- down_bias: float32 [512], replicated, may hold values from -3 to 3
Outputs:
- output: bfloat16 [2, 1536, 8, 512], P('grp', 'samp')
- grad_tokens: float32 [2, 1536, 8, 512], P('grp', 'samp')
- grad_first_gain: float32 [512], P('samp')
- grad_first_shift: float32 [512], P('samp')
- grad_sample_qkv: float32 [512, 1536], P('samp')
- grad_sample_out: float32 [512, 512], P('samp')
- grad_second_gain: float32 [512], P('samp')
- grad_second_shift: float32 [512], P('samp')
- grad_feature_qkv: float32 [512, 1536], P('samp')
- grad_feature_out: float32 [512, 512], P('samp')
- grad_third_gain: float32 [512], P('samp')
- grad_third_shift: float32 [512], P('samp')
- grad_up_weight: float32 [512, 2048], P('samp')
- grad_up_bias: float32 [2048], P('samp')
- grad_down_weight: float32 [2048, 512], P('samp')
- grad_down_bias: float32 [512], P('samp')
Inputs may be any that keep to these rules, and one draw needn't show every extreme that they name: `segments`: -1 marks a padding slot, other values name a sample's task.
All inputs are finite; a program needn't handle non-finite values.
Results may differ from a plain program's by a relative error of at most 0.023.
Values may be sent and summed in bfloat16 or wider, within the bound.
No kernel may reach another device: no remote copies, remote signals or barrier semaphores. Data moves between devices by JAX's collectives and lax.ppermute only.
A program may use at most 512 MiB of HBM per device.

v0:
```python
import functools
import math

import jax
import jax.numpy as jnp
from jax import lax
from jax.experimental import pallas as pl
from jax.experimental.pallas import tpu as pltpu
from jax.sharding import PartitionSpec as P

H = 8
HD = 64
EPSILON = 1e-05
SCALING = 0.125
NEGATIVE = -1e30
BF = jnp.bfloat16
F32 = jnp.float32
TILE = 256
FT = 512
PB = 512
KB = 256
QB = 256
TQ = 256
TK = 256
LANES = 128
PAD = 8
GELU_C = math.sqrt(2.0 / math.pi)
GELU_A = 0.044715
MIB = 1024 * 1024
CLASSES = 5


def dot(a, b):
    return jnp.dot(a, b, preferred_element_type=F32)


def dot_nt(a, b):
    return lax.dot_general(a, b, (((1,), (1,)), ((), ())), preferred_element_type=F32)


def dot_tn(a, b):
    return lax.dot_general(a, b, (((0,), (0,)), ((), ())), preferred_element_type=F32)


def ln_parts(v):
    c = v - jnp.mean(v, -1, keepdims=True)
    r = lax.rsqrt(jnp.mean(c * c, -1, keepdims=True) + EPSILON)
    return c * r, r


def ln_back(dh, n, r, g):
    e = dh * g
    return r * (e - jnp.mean(e, -1, keepdims=True) - n * jnp.mean(e * n, -1, keepdims=True))


def flip(v):
    return jnp.transpose(v)


def head_columns(w, r, cl, which):
    first = which * (w.shape[1] // 3) + r * cl
    return w[:, pl.ds(pl.multiple_of(first, LANES), cl)]


def lay(scr, v):
    for a in range(scr.shape[0]):
        scr[a] = v[:, a * LANES : (a + 1) * LANES]


def lift(scr):
    return jnp.concatenate([scr[a] for a in range(scr.shape[0])], -1)


def take(scr, first, count, step):
    return jnp.concatenate(
        [scr[a, pl.ds(first, count, stride=step), :] for a in range(scr.shape[0])], -1
    )


def place(scr, first, count, step, v):
    for a in range(scr.shape[0]):
        scr[a, pl.ds(first, count, stride=step), :] = v[:, a * LANES : (a + 1) * LANES]


def iota(shape, dim):
    return lax.broadcasted_iota(jnp.int32, shape, dim).astype(F32)


def call(fn, outs, scratch, *args, smem=(), smem_out=(), hbm=(), hbm_out=(), vmem=16):
    def spec(space):
        return pl.BlockSpec(memory_space=space)

    def place_of(i, scalars, far):
        return spec(pltpu.SMEM if i in scalars else pl.ANY if i in far else pltpu.VMEM)

    in_specs = [place_of(i, smem, hbm) for i in range(len(args))]
    out_specs = [place_of(i, smem_out, hbm_out) for i in range(len(outs))]
    return pl.pallas_call(
        fn,
        out_shape=[jax.ShapeDtypeStruct(*o) for o in outs],
        in_specs=in_specs,
        out_specs=out_specs,
        scratch_shapes=scratch,
        compiler_params=pltpu.CompilerParams(vmem_limit_bytes=vmem * MIB),
        cost_estimate=pl.CostEstimate(flops=0, bytes_accessed=0, transcendentals=0),
    )(*args)


def pack_kernel(tok, seg, out, scr):
    count, feats, width = tok.shape
    lay(scr, tok[...].astype(F32).reshape(count * feats, width))
    row = seg[...].astype(F32)
    for f in range(feats):
        out[f, :count, :] = take(scr, f, count, feats).astype(BF)
        out[f, count:, :] = jnp.zeros((PAD, width), BF)
        out[f, count:, :count] = jnp.broadcast_to(row, (PAD, count)).astype(BF)


def codes(pos, starts):
    cls = jnp.zeros_like(pos)
    for st in starts:
        cls = cls + jnp.where(pos >= st, 1.0, 0.0)
    return jnp.where(cls >= CLASSES - 1, pos + CLASSES, cls)


def tile_range(start_ref, first, size, tile):
    last = first + size - 1
    lo = jnp.int32(0)
    hi = start_ref[1]
    for c in range(1, CLASSES - 1):
        st = start_ref[c]
        lo = jnp.where(first >= st, st, lo)
        hi = jnp.where(last >= st, start_ref[c + 1], hi)
    pad = start_ref[CLASSES - 1]
    lo = jnp.where(first >= pad, first, lo)
    hi = jnp.where(last >= pad, first + size, hi)
    return lo // tile, (hi + tile - 1) // tile


def permute_block(rank_row, first, rows, total):
    pos = iota((rows, LANES), 0) + first.astype(F32)
    parts = []
    for j in range(total // LANES):
        hit = rank_row[0:1, j * LANES : (j + 1) * LANES] == pos
        parts.append(jnp.where(hit, 1.0, 0.0).astype(BF))
    return jnp.concatenate(parts, -1)


def unpermute_block(rank_col, total):
    rows = rank_col.shape[0]
    parts = []
    for j in range(total // LANES):
        pos = iota((1, LANES), 1) + float(j * LANES)
        parts.append(jnp.where(rank_col == pos, 1.0, 0.0).astype(BF))
    return jnp.concatenate(parts, -1)


def fwd_kernel(hpd, hl, r_ref, *refs):
    xparts = refs[:hpd]
    (g1, b1, w_in) = refs[hpd : hpd + 3]
    (o_send, xs_out, ot_out, lse_out, rank_row, rank_col, start_ref) = refs[hpd + 3 : hpd + 10]
    (x_scr, seg_scr, qtz, k_scr, vt, o_scr, code_col, code_row, acc, top, s_scr) = refs[
        hpd + 10 : hpd + 21
    ]
    wqt, wvt = refs[hpd + 21 :]
    feats = xparts[0].shape[0]
    count = xparts[0].shape[1] - PAD
    total = x_scr.shape[0]
    cl = hl * HD
    r = r_ref[0]
    chunks = total // LANES
    wqt[...] = flip(head_columns(w_in, r, cl, 0)) * BF(SCALING)
    wvt[...] = flip(head_columns(w_in, r, cl, 2))

    for s in range(hpd):
        for k in range(feats):
            at = (s * feats + k) * count
            x_scr[at : at + count, :] = xparts[s][k, :count, :]
            row = xparts[s][k, count : count + PAD, :LANES].astype(F32)[0:1]
            col = jnp.transpose(jnp.broadcast_to(row, (LANES, LANES)))
            seg_scr[at : at + count, :] = col[:count, :]

    seg = seg_scr[...]
    cls = jnp.where(seg < 0.0, float(CLASSES - 1), seg)
    seg_scr[...] = cls * 8192.0 + iota((total, LANES), 0)
    key_rows = []
    for j in range(chunks):
        blk = seg_scr[j * LANES : (j + 1) * LANES, :]
        key_rows.append(jnp.transpose(blk)[0:8, :])

    def count_less(i, carry):
        blk = seg_scr[pl.ds(pl.multiple_of(i * 64, 64), 64), :]
        out = []
        for j in range(chunks):
            less = jnp.where(blk < key_rows[j][0:1], 1.0, 0.0)
            out.append(carry[j] + jnp.sum(less.reshape(8, 8, LANES), 0))
        return tuple(out)

    ranks = lax.fori_loop(
        0, total // 64, count_less, tuple(jnp.zeros((8, LANES), F32) for _ in range(chunks))
    )
    for j in range(chunks):
        row = jnp.sum(ranks[j], 0, keepdims=True)
        rank_row[:, j * LANES : (j + 1) * LANES] = jnp.broadcast_to(row, (8, LANES))
        rank_col[j * LANES : (j + 1) * LANES, :] = jnp.transpose(
            jnp.broadcast_to(row, (LANES, LANES))
        )
    starts = []
    keys = jnp.concatenate([k[0:1] for k in key_rows], 0)
    for c in range(1, CLASSES):
        st = jnp.sum(jnp.where(keys < c * 8192.0, 1.0, 0.0))
        starts.append(st)
        start_ref[c] = st.astype(jnp.int32)
    start_ref[0] = jnp.int32(0)
    for c in range(CLASSES, 8):
        start_ref[c] = jnp.int32(total)
    code_col[...] = codes(iota((total, LANES), 0), starts)
    code_row[...] = codes(iota((8, total), 1), starts)

    qtz[...] = jnp.zeros_like(qtz)
    ones = jnp.where(iota((16, total), 0) == 0.0, 1.0, 0.0).astype(BF)
    for h in range(hl):
        vt[h, HD:, :] = ones

    def project(b, _):
        at = pl.multiple_of(b * PB, PB)
        block = dot(permute_block(rank_row, at, PB, total), x_scr[...])
        xs_out[pl.ds(at, PB), :] = block.astype(BF)
        n, _r = ln_parts(block)
        h1 = (n * g1[...] + b1[...]).astype(BF)
        qt = dot_nt(wqt[...], h1).astype(BF)
        k_scr[pl.ds(at, PB), :] = dot(h1, head_columns(w_in, r, cl, 1)).astype(BF)
        vv = dot_nt(wvt[...], h1).astype(BF)
        for h in range(hl):
            sub = (h % 2) * HD
            qtz[h, sub : sub + HD, pl.ds(at, PB)] = qt[h * HD : (h + 1) * HD]
            vt[h, :HD, pl.ds(at, PB)] = vv[h * HD : (h + 1) * HD]
        return 0

    lax.fori_loop(0, total // PB, project, 0)

    def attend(b, _):
        at = pl.multiple_of(b * TQ, TQ)
        t0, t1 = tile_range(start_ref, at, TQ, TK)
        acc[...] = jnp.zeros_like(acc)
        top[...] = jnp.full_like(top, NEGATIVE)
        crow = code_row[0:1, pl.ds(at, TQ)]

        def score(t, _):
            kt = pl.multiple_of(t * TK, TK)
            ccol = code_col[pl.ds(kt, TK), :]
            ccol = jnp.concatenate([ccol] * (TQ // LANES), -1)
            seen = ccol == crow
            for h in range(hl):
                pair = (h // 2) * LANES
                s = dot(k_scr[pl.ds(kt, TK), pair : pair + LANES], qtz[h, :, pl.ds(at, TQ)])
                s = jnp.where(seen, s, NEGATIVE)
                s_scr[h, pl.ds(kt, TK), :] = s
                top[h] = jnp.maximum(top[h], jnp.max(s.reshape(TK // 8, 8, TQ), 0))
            return 0

        lax.fori_loop(t0, t1, score, 0)
        for h in range(hl):
            top[h] = jnp.broadcast_to(jnp.max(top[h], 0, keepdims=True), (8, TQ))

        def mix(t, _):
            kt = pl.multiple_of(t * TK, TK)
            for h in range(hl):
                p = jnp.exp(s_scr[h, pl.ds(kt, TK), :] - top[h, 0:1, :]).astype(BF)
                acc[h] += dot(vt[h, :, pl.ds(kt, TK)], p)
            return 0

        lax.fori_loop(t0, t1, mix, 0)
        outs = []
        for h in range(hl):
            total_h = acc[h, HD : HD + 1, :]
            outs.append(acc[h, :HD, :] / total_h)
            lse_out[h : h + 1, pl.ds(at, TQ)] = top[h, 0:1, :] + jnp.log(total_h)
        ot = jnp.concatenate(outs, 0)
        ot_out[:, pl.ds(at, TQ)] = ot.astype(BF)
        o_scr[pl.ds(at, TQ), :] = jnp.transpose(ot).astype(BF)
        return 0

    lax.fori_loop(0, total // TQ, attend, 0)

    group = feats // 2
    for blk in range(total // (group * count)):
        at = blk * group * count
        hot = unpermute_block(rank_col[at : at + group * count, :], total)
        o = dot(hot, o_scr[...]).astype(BF)
        for j in range(group):
            s, k = divmod(blk * group + j, feats)
            dest = k * hpd + lax.rem(r - s + hpd, hpd)
            o_send[dest] = o[j * count : (j + 1) * count]


def prep_kernel(
    hl,
    r_ref,
    xs,
    g1,
    b1,
    w_in,
    k_out,
    v_out,
    kt_out,
    qtz,
    nt,
    wqt,
    wkt,
):
    total = xs.shape[0]
    cl = hl * HD
    r = r_ref[0]
    wqt[...] = flip(head_columns(w_in, r, cl, 0)) * BF(SCALING)
    wkt[...] = flip(head_columns(w_in, r, cl, 1))
    qtz[...] = jnp.zeros_like(qtz)

    def project(b, _):
        at = pl.multiple_of(b * PB, PB)
        n, _r = ln_parts(xs[pl.ds(at, PB), :].astype(F32))
        h1 = (n * g1[...] + b1[...]).astype(BF)
        nt[:, pl.ds(at, PB)] = jnp.transpose(n.astype(BF))
        qt = dot_nt(wqt[...], h1).astype(BF)
        k_out[pl.ds(at, PB), :] = dot(h1, head_columns(w_in, r, cl, 1)).astype(BF)
        v_out[pl.ds(at, PB), :] = dot(h1, head_columns(w_in, r, cl, 2)).astype(BF)
        kt_out[:, pl.ds(at, PB)] = dot_nt(wkt[...], h1).astype(BF)
        for h in range(hl):
            sub = (h % 2) * HD
            qtz[h, sub : sub + HD, pl.ds(at, PB)] = qt[h * HD : (h + 1) * HD]
        return 0

    lax.fori_loop(0, total // PB, project, 0)


def plus(a, b):
    return (a.astype(F32) + b.astype(F32)).astype(BF)


def first_sums(x_ref, y_ref, a_keep, a_got, c_keep, c_got, a_mine, a_other, c_mine, c_other):
    half = a_mine.shape[1]
    mine = pl.multiple_of(x_ref[0] * half, half)
    other = pl.multiple_of((1 - x_ref[0]) * half, half)

    def step(i, _):
        for ref, first in ((a_mine, mine), (a_other, other)):
            ref[i] = plus(a_keep[i, pl.ds(first, half), :], a_got[i, pl.ds(first, half), :])
        return 0

    lax.fori_loop(0, a_mine.shape[0], step, 0)
    split_y(y_ref[0], c_keep, c_got, c_mine, c_other)


def split_y(y, keep, got, mine, other):
    def step(i, _):
        for ref, at in ((mine, 2 * i + y), (other, 2 * i + 1 - y)):
            ref[i] = plus(keep[at], got[at])
        return 0

    lax.fori_loop(0, mine.shape[0], step, 0)


def top_split(z_ref, keep, got, mine, other):
    chunks = mine.shape[0]
    top = z_ref[0] // chunks
    for j in range(chunks):
        mine[j] = plus(keep[top * chunks + j], got[top * chunks + j])
        other[j] = plus(keep[(1 - top) * chunks + j], got[(1 - top) * chunks + j])


def middle_sums(z_ref, a_keep, a_got, c_keep, c_got, *pieces):
    count = a_keep.shape[0]
    pick_z(z_ref, a_keep, a_got, *pieces[:count])
    for c, ref in enumerate(pieces[count:]):
        at = lax.bitwise_xor(lax.rem(z_ref[0], count // 2), c)
        ref[...] = plus(c_keep[at], c_got[at])


def add_all(terms):
    total = terms[0].astype(F32)
    for term in terms[1:]:
        total = total + term.astype(F32)
    return total.astype(BF)


def pick_y(y_ref, keep, got, mine, other):
    split_y(y_ref[0], keep, got, mine, other)


def pick_z(z_ref, keep, got, *pieces):
    for c, ref in enumerate(pieces):
        at = lax.bitwise_xor(z_ref[0], c)
        ref[...] = plus(keep[at], got[at])


def sum_kernel(*refs):
    refs[-1][...] = add_all([ref[...] for ref in refs[:-1]])


def bwd_kernel(
    hpd,
    hl,
    r_ref,
    start_ref,
    do_recv,
    k_in,
    v_in,
    kt_in,
    qtz,
    ot,
    lse,
    rank_row,
    dt_out,
    do_scr,
    dotz,
    dots,
    code_col,
    code_row,
    dq_acc,
    dk_acc,
    dv_acc,
    p_scr,
    ds_scr,
    pairs,
):
    feats = do_recv.shape[0] // hpd
    count = do_recv.shape[1]
    total = do_scr.shape[0]
    cl = hl * HD
    r = r_ref[0]

    for s in range(hpd):
        for k in range(feats):
            at = (s * feats + k) * count
            do_scr[at : at + count, :] = do_recv[k * hpd + lax.rem(r - s + hpd, hpd)]
    starts = [start_ref[c].astype(F32) for c in range(1, CLASSES)]
    code_col[...] = codes(iota((total, LANES), 0), starts)
    code_row[...] = codes(iota((8, total), 1), starts)
    dotz[...] = jnp.zeros_like(dotz)

    def arrange(b, _):
        at = pl.multiple_of(b * PB, PB)
        block = jnp.transpose(dot(permute_block(rank_row, at, PB, total), do_scr[...]))
        prod = block * ot[:, pl.ds(at, PB)].astype(F32)
        for h in range(hl):
            sub = (h % 2) * HD
            rows = slice(h * HD, (h + 1) * HD)
            dotz[h, sub : sub + HD, pl.ds(at, PB)] = block[rows].astype(BF)
            dots[h : h + 1, pl.ds(at, PB)] = jnp.sum(prod[rows], 0, keepdims=True)
        return 0

    lax.fori_loop(0, total // PB, arrange, 0)
    dq_acc[...] = jnp.zeros_like(dq_acc)
    dk_acc[...] = jnp.zeros_like(dk_acc)
    dv_acc[...] = jnp.zeros_like(dv_acc)

    def list_keys(b, filled):
        t0, t1 = tile_range(start_ref, b * KB, KB, QB)

        def put(t, i):
            pairs[i] = b * 4096 + t
            return i + 1

        return lax.fori_loop(t0, t1, put, filled)

    filled = lax.fori_loop(0, total // KB, list_keys, jnp.int32(0))

    def places(i):
        b, t = pairs[i] // 4096, lax.rem(pairs[i], 4096)
        return pl.ds(pl.multiple_of(b * KB, KB), KB), pl.ds(pl.multiple_of(t * QB, QB), QB)

    def scores(i):
        kt, at = places(i)
        ccol = code_col[kt, :]
        seen = jnp.concatenate([ccol] * (QB // LANES), -1) == code_row[0:1, at]
        for h in range(hl):
            cols = slice(h // 2 * LANES, (h // 2 + 1) * LANES)
            s = dot(k_in[kt, cols], qtz[h, :, at])
            p = jnp.where(seen, jnp.exp(s - lse[h : h + 1, at]), 0.0)
            dp = dot(v_in[kt, cols], dotz[h, :, at])
            p_scr[h] = p.astype(BF)
            ds_scr[h] = (p * (dp - dots[h : h + 1, at])).astype(BF)

    def collect(i):
        kt, at = places(i)
        for h in range(hl):
            rows = slice(h * HD, (h + 1) * HD)
            own = slice((h % 2) * HD, (h % 2 + 1) * HD)
            ds = ds_scr[h]
            dv_acc[rows, kt] += dot_nt(dotz[h, own, at], p_scr[h])
            dk_acc[rows, kt] += dot_nt(qtz[h, own, at], ds)
            dq_acc[rows, at] += dot(kt_in[rows, kt], ds)

    def step(i, _):
        scores(i)
        collect(i)
        return 0

    lax.fori_loop(0, filled, step, 0)
    dt_out[:cl, :] = (dq_acc[...] * SCALING).astype(BF)
    dt_out[cl : 2 * cl, :] = dk_acc[...].astype(BF)
    dt_out[2 * cl :, :] = dv_acc[...].astype(BF)


def dh_kernel(hpd, r_ref, dt, w_in, rank_col, *refs):
    dh_outs, dht = refs[:-1], refs[-1]
    part, count, width = dh_outs[0].shape
    cuts = len(dh_outs) // hpd
    feats = cuts * part
    total = dt.shape[1]
    cl = dt.shape[0] // 3
    w3 = jnp.concatenate([head_columns(w_in, r_ref[0], cl, j) for j in range(3)], 1)
    for b in range(total // PB):
        at = slice(b * PB, (b + 1) * PB)
        dht[:, at] = dot(w3, dt[:, at]).astype(BF)
    group = feats // 2
    for blk in range(total // (group * count)):
        at = blk * group * count
        hot = unpermute_block(rank_col[at : at + group * count, :], total)
        o = dot_nt(hot, dht[...]).astype(BF)
        for j in range(group):
            s, k = divmod(blk * group + j, feats)
            dh_outs[cuts * s + k // part][k % part] = o[j * count : (j + 1) * count]


SUB = 16
CUTS = 4


def q_rows(cl, width):
    return SUB * (-(-6 * cl // width)) + SUB


def dw_kernel(r_ref, x_ref, y_ref, z_ref, dt, nt, w_in, g1, b1, *refs):
    x = x_ref[0]
    width, total = nt.shape
    cols = dt.shape[0]
    cl = cols // 3
    a_keep, a_got, c_keep, c_got, q_keep, q_send, a_mine, a_other, c_mine, c_other = refs[:10]
    m_scr, dw_scr = refs[10:]
    split_y(y_ref[0], a_keep, a_got, a_mine, a_other)
    top_split(z_ref, c_keep, c_got, c_mine, c_other)
    feats = q_keep.shape[0]
    for c in range(3):
        rows = slice(c * cl, (c + 1) * cl)
        m_scr[:, rows] = dot_nt(nt[...], dt[rows, :])
    ones = jnp.ones((8, total), BF)
    sums_row = dot_nt(ones, dt[...])[0:1]
    gcol = jnp.transpose(jnp.broadcast_to(g1[...], (LANES, width)))
    bcol = jnp.transpose(jnp.broadcast_to(b1[...], (LANES, width)))
    gg = jnp.zeros((width, LANES), F32)
    gb = jnp.zeros((width, LANES), F32)
    for j in range(cols // LANES):
        lanes = slice(j * LANES, (j + 1) * LANES)
        first = (j * LANES // cl) * width + r_ref[0] * cl + j * LANES % cl
        w = w_in[:, pl.ds(pl.multiple_of(first, LANES), LANES)].astype(F32)
        m = m_scr[:, lanes]
        gg = gg + w * m
        gb = gb + w * sums_row[:, lanes]
        dw_scr[:, lanes] = (m * gcol + bcol * sums_row[:, lanes]).astype(BF)
    gg = jnp.sum(jnp.transpose(gg), 0, keepdims=True)
    gb = jnp.sum(jnp.transpose(gb), 0, keepdims=True)
    vec = jnp.concatenate([gg, gb, jnp.zeros((SUB - 2, width), F32)], 0).astype(BF)
    per = width // cl
    last = q_keep.shape[1] - SUB
    for e in range(feats):
        for ref, side in ((q_keep, x), (q_send, 1 - x)):
            for s in range(6):
                j, b = divmod(s, 2)
                src = pl.multiple_of((e * 4 + b) * SUB + side * 2 * SUB, SUB)
                to = (s // per) * SUB
                ref[e, to : to + SUB, (s % per) * cl : (s % per + 1) * cl] = dw_scr[
                    pl.ds(src, SUB), j * cl : (j + 1) * cl
                ]
            used = 6 % per
            if used:
                ref[e, last - SUB : last, used * cl :] = jnp.zeros((SUB, width - used * cl), BF)
            ref[e, last:, :] = vec


def gather_kernel(hpd, r_ref, x_ref, *refs):
    same, other = refs[:hpd], refs[hpd : 2 * hpd]
    a_side, a_pair, c_sum, c_pair = refs[2 * hpd : 2 * hpd + 4]
    out, vec, down, up, fqkv, fout, sout, vectors = refs[2 * hpd + 4 :]
    piece = out.shape[0]
    rows, width = same[0].shape
    cl = width // hpd
    r, x = r_ref[0], x_ref[0]
    blocks = piece // SUB
    first = lax.rem(r * blocks, 2)
    from_same = r * blocks // 2 == x
    for s in range(hpd):
        owner = lax.rem(r - s + hpd, hpd)
        for j in range(3):
            lo = 2 * j // hpd * SUB
            to = pl.ds(pl.multiple_of(j * width + owner * cl, LANES), cl)
            for b in range(blocks):
                col = pl.multiple_of((2 * j % hpd + first + b) * cl, LANES)
                at = (slice(lo, lo + SUB), pl.ds(col, cl))
                picked = jnp.where(from_same, same[s][at].astype(F32), other[s][at].astype(F32))
                out[b * SUB : (b + 1) * SUB, to] = picked
    total = same[0][rows - SUB : rows, :].astype(F32)
    for s in range(1, hpd):
        total = total + same[s][rows - SUB : rows, :].astype(F32)
    vec[...] = total[:8]

    down[...] = jnp.where(x == 0, a_side[...].astype(F32), a_pair[...].astype(F32))

    def both(first, size):
        at = slice(first, first + size)
        return c_sum[at, :].astype(F32) + c_pair[at, :].astype(F32)

    for b in range(up.shape[1] // width):
        at = slice(b * piece, (b + 1) * piece)
        block = jnp.where(x == 0, a_pair[at, :].astype(F32), a_side[at, :].astype(F32))
        up[:, b * width : (b + 1) * width] = block
    base = 0
    for ref in (fqkv, fout, sout):
        for b in range(ref.shape[1] // width):
            ref[:, b * width : (b + 1) * width] = both(base, piece)
            base += piece
    vectors[...] = both(base, vectors.shape[0])


def norm_kernel(hpd, *refs):
    parts = refs[:-5]
    x, g1, q_keep, q_got, out = refs[-5:]
    part, count, _w = parts[0].shape
    cuts = len(parts) // hpd
    feats = cuts * part
    for k in range(feats):
        dh = parts[k // part][k % part].astype(F32)
        for s in range(1, hpd):
            dh = dh + parts[cuts * s + k // part][k % part].astype(F32)
        n, r = ln_parts(x[k, :count, :].astype(F32))
        out[k, :count, :] = ln_back(dh, n, r, g1[...]).astype(BF)
        out[k, count:, :] = add_all((q_keep[k], q_got[k]))


def final_kernel(dx1, both, out, q_sum, scr):
    feats = both.shape[0]
    count, _f, width = out.shape
    q_sum[...] = add_all([both[k, count:, :] for k in range(feats)])
    for f in range(feats):
        val = dx1[f * count : (f + 1) * count, :] + both[f, :count, :].astype(F32)
        place(scr, f, count, feats, val)
    out[...] = lift(scr).reshape(count, feats, width)


def rows_kernel(
    hpd,
    me_ref,
    o_recv,
    xt,
    cot_hbm,
    g2,
    b2,
    g3,
    b3,
    ub,
    db,
    wso_hbm,
    wfq_hbm,
    wfo_hbm,
    wup_hbm,
    wdn_hbm,
    *refs,
):
    outs_hbm, scratch = refs[:7], refs[7:-2]
    (wso, wfq, wfo, wup, wdn, cot), scratch = scratch[:6], scratch[6:]
    outs_vmem, scratch = scratch[:7], scratch[7:]
    out, dx1, do_send, a_keep, a_send, b_keep, b_send = outs_vmem
    (
        wide,
        ct,
        o1,
        x1,
        h2,
        qkv,
        o2,
        x2,
        h3,
        u,
        dz,
        dx2,
        do2,
        dqkv,
        pscr,
        tr,
        wblk,
        ubg,
        wdn_scr,
    ) = scratch
    in_sem, out_sem = refs[-2:]
    loads = [
        pltpu.make_async_copy(src, dst, in_sem.at[i])
        for i, (src, dst) in enumerate(
            (
                (cot_hbm, cot),
                (wso_hbm, wso),
                (wfq_hbm, wfq),
                (wfo_hbm, wfo),
                (wup_hbm, wup),
                (wdn_hbm, wdn),
            )
        )
    ]
    for load in loads:
        load.start()
    stores = [
        pltpu.make_async_copy(src, dst, out_sem.at[i])
        for i, (src, dst) in enumerate(zip(outs_vmem, outs_hbm))
    ]
    feats = xt.shape[0]
    count = xt.shape[1] - PAD
    width = xt.shape[2]
    rows = feats * count
    hidden = wup.shape[1]
    n = o_recv.shape[0]
    cl = o_recv.shape[2]
    half = rows // 2
    me = me_ref[0]
    lane = iota((1, LANES), 1)
    part = 16
    tiles = count // part
    size = feats * part

    loads[0].wait()
    lay(wide, cot[...].astype(F32).reshape(rows, width))
    for f in range(feats):
        ct[f * count : (f + 1) * count, :] = take(wide, f, count, feats).astype(BF)
        for c in range(hpd):
            o1[f * count : (f + 1) * count, c * cl : (c + 1) * cl] = o_recv[f * hpd + c]

    loads[1].wait()
    for b in range(2):
        at = slice(b * half, (b + 1) * half)
        x = xt[b * feats // 2 : (b + 1) * feats // 2, :count, :].astype(F32).reshape(half, width)
        v = x + dot(o1[at, :], wso[...])
        x1[at, :] = v
        nn, _r = ln_parts(v)
        h2[at, :] = (nn * g2[...] + b2[...]).astype(BF)

    loads[2].wait()
    qkv3 = qkv

    def qkv_step(c, _):
        cols = pl.ds(pl.multiple_of(c * TILE, TILE), TILE)
        scale = jnp.where(c < width // TILE, SCALING, 1.0)
        y = dot(h2[...], wfq[:, cols])
        qkv3[:, :, cols] = (y * scale).astype(BF).reshape(feats, count, TILE)
        return 0

    lax.fori_loop(0, 3 * width // TILE, qkv_step, 0)

    ri = lax.broadcasted_iota(jnp.int32, (2 * size, size), 0)
    ci = lax.broadcasted_iota(jnp.int32, (2 * size, size), 1)
    same = lax.rem(ri, part) == lax.rem(ci, part)
    low_lane = jnp.where(iota((1, LANES), 1) < HD, 1.0, 0.0).astype(BF)
    high_lane = jnp.where(iota((1, LANES), 1) < HD, 0.0, 1.0).astype(BF)

    def tile_of(ref, at, lo):
        return ref[:, at, lo : lo + LANES].reshape(size, LANES)

    def by_head(v):
        return jnp.concatenate([v * low_lane, v * high_lane], 0)

    def by_head_t(v):
        vt = jnp.transpose(v)
        zero = jnp.zeros((HD, size), BF)
        return jnp.concatenate(
            [jnp.concatenate([vt[:HD], zero], 0), jnp.concatenate([zero, vt[HD:]], 0)], 1
        )

    def side(v):
        return jnp.concatenate([v[:size], v[size:]], 1)

    def per_head(v, fn):
        return jnp.concatenate(
            [jnp.broadcast_to(fn(v[i * size : (i + 1) * size]), (size, size)) for i in (0, 1)], 0
        )

    def feat_fwd(t, _):
        at = pl.ds(pl.multiple_of(t * part, part), part)
        for p2 in range(H // 2):
            lo = p2 * LANES
            q = tile_of(qkv3, at, lo)
            k = tile_of(qkv3, at, width + lo)
            v = tile_of(qkv3, at, 2 * width + lo)
            s = jnp.where(same, dot_nt(by_head(k), q), NEGATIVE)
            e = jnp.exp(s - per_head(s, lambda w: jnp.max(w, 0, keepdims=True)))
            p = (e * per_head(e, lambda w: 1.0 / jnp.sum(w, 0, keepdims=True))).astype(BF)
            pscr[t, p2] = p
            ot = dot(by_head_t(v), p)
            o2[:, at, lo : lo + LANES] = jnp.transpose(ot).astype(BF).reshape(feats, part, LANES)
        return 0

    lax.fori_loop(0, tiles, feat_fwd, 0, unroll=2)

    loads[3].wait()
    for b in range(2):
        at = slice(b * half, (b + 1) * half)
        o = o2[b * feats // 2 : (b + 1) * feats // 2, :, :].reshape(half, width)
        v = x1[at, :] + dot(o, wfo[...])
        x2[at, :] = v
        nn, _r = ln_parts(v)
        h3[at, :] = (nn * g3[...] + b3[...]).astype(BF)

    loads[4].wait()
    loads[5].wait()

    def ffn(c, _):
        cols = pl.ds(pl.multiple_of(c * FT, FT), FT)
        total = jnp.zeros((8, FT), F32)
        for b in range(2):
            at = slice(b * half, (b + 1) * half)
            z = dot(h3[at, :], wup[:, cols]) + ub[0:1, cols]
            w = GELU_C * GELU_A * (z * z) + GELU_C
            cdf = 0.5 * jnp.tanh(z * w) + 0.5
            g = z * cdf
            u[at, cols] = g.astype(BF)
            slope = cdf + g * (1.0 - cdf) * (6.0 * w - 4.0 * GELU_C)
            d = dot_nt(ct[at, :], wdn[cols, :]) * slope
            dz[at, cols] = d.astype(BF)
            total = total + jnp.sum(d.reshape(half // 8, 8, FT), 0)
        ubg[:, cols] = total
        return 0

    lax.fori_loop(0, hidden // FT, ffn, 0)

    vectors = []
    gg = jnp.zeros((1, width), F32)
    gb = jnp.zeros((1, width), F32)
    gd = jnp.zeros((1, width), F32)
    for b in range(2):
        at = slice(b * half, (b + 1) * half)
        y = x2[at, :] + dot(u[at, :], wdn[...]) + db[...]
        for j in range(feats // 2):
            f = b * (feats // 2) + j
            place(wide, f, count, feats, y[j * count : (j + 1) * count])
        dh = dot_nt(dz[at, :], wup[...])
        nn, r = ln_parts(x2[at, :])
        c = ct[at, :].astype(F32)
        gg = gg + jnp.sum(dh * nn, 0, keepdims=True)
        gb = gb + jnp.sum(dh, 0, keepdims=True)
        gd = gd + jnp.sum(c, 0, keepdims=True)
        v = c + ln_back(dh, nn, r, g3[...])
        dx2[at, :] = v
        do2[b * feats // 2 : (b + 1) * feats // 2, :, :] = (
            dot_nt(v.astype(BF), wfo[...]).astype(BF).reshape(feats // 2, count, width)
        )
    out[...] = lift(wide).reshape(count, feats, width).astype(BF)
    stores[0].start()
    vectors = [gg, gb, gd]

    core = lax.rem(me, 2)

    def slot(pos):
        at, other = divmod(pos, 2)
        refs = (a_send, b_send) if other else (a_keep, b_keep)
        return refs, at, 2 * at + (1 - core if other else core)

    piece = width // n
    fpiece = hidden // n

    def spread(group, base):
        for pos in range(n):
            refs, at, d = slot(pos)
            src = pl.multiple_of(d * piece, piece)
            refs[group][at, base : base + piece, :] = wblk[pl.ds(src, piece), :]

    base = 0
    for b in range(hidden // width):
        tr[...] = flip(u[:, b * width : (b + 1) * width])
        wdn_scr[b * width : (b + 1) * width, :] = dot(tr[...], ct[...]).astype(BF)
    for pos in range(n):
        refs, at, d = slot(pos)
        src = pl.multiple_of(d * fpiece, fpiece)
        refs[0][at, base : base + fpiece, :] = wdn_scr[pl.ds(src, fpiece), :]
    base += fpiece
    tr[...] = flip(h3[...])
    for b in range(hidden // width):
        wblk[...] = dot(tr[...], dz[:, b * width : (b + 1) * width]).astype(BF)
        spread(0, base)
        base += piece
    stores[3].start()
    stores[4].start()

    def feat_bwd(t, _):
        at = pl.ds(pl.multiple_of(t * part, part), part)
        for p2 in range(H // 2):
            lo = p2 * LANES
            q = tile_of(qkv3, at, lo)
            k = tile_of(qkv3, at, width + lo)
            v = tile_of(qkv3, at, 2 * width + lo)
            g = tile_of(do2, at, lo)
            p = pscr[t, p2]
            pf = p.astype(F32)
            dp = dot_nt(by_head(v), g)
            ds = pf * (dp - per_head(pf * dp, lambda w: jnp.sum(w, 0, keepdims=True)))
            ds = ds.astype(BF)
            dv = dot(side(p), by_head(g))
            dk = dot(side(ds), by_head(q))
            dq = jnp.transpose(dot(by_head_t(k), ds)) * SCALING
            for j, d in enumerate((dq, dk, dv)):
                dqkv[:, at, j * width + lo : j * width + lo + LANES] = d.astype(BF).reshape(
                    feats, part, LANES
                )
        return 0

    lax.fori_loop(0, tiles, feat_bwd, 0, unroll=2)

    gg = jnp.zeros((1, width), F32)
    gb = jnp.zeros((1, width), F32)
    for b in range(2):
        at = slice(b * half, (b + 1) * half)
        d = dqkv[b * feats // 2 : (b + 1) * feats // 2, :, :].reshape(half, 3 * width)
        dh = dot_nt(d, wfq[...])
        nn, r = ln_parts(x1[at, :])
        gg = gg + jnp.sum(dh * nn, 0, keepdims=True)
        gb = gb + jnp.sum(dh, 0, keepdims=True)
        v = dx2[at, :] + ln_back(dh, nn, r, g2[...])
        dx1[at, :] = v
        g = dot_nt(v.astype(BF), wso[...]).astype(BF)
        for j in range(feats // 2):
            f = b * (feats // 2) + j
            for c in range(hpd):
                do_send[f * hpd + c] = g[j * count : (j + 1) * count, c * cl : (c + 1) * cl]
    stores[1].start()
    stores[2].start()
    vectors = [gg, gb] + vectors

    base = 0
    tr[...] = flip(h2[...])
    for b in range(3):
        d = dqkv[:, :, b * width : (b + 1) * width].reshape(rows, width)
        wblk[...] = dot(tr[...], d).astype(BF)
        spread(1, base)
        base += piece
    tr[...] = flip(o2[...].reshape(rows, width))
    wblk[...] = dot(tr[...], dx2[...].astype(BF)).astype(BF)
    spread(1, base)
    base += piece
    tr[...] = flip(o1[...])
    wblk[...] = dot(tr[...], dx1[...].astype(BF)).astype(BF)
    spread(1, base)
    base += piece
    ubs = jnp.sum(ubg[...], 0, keepdims=True)
    vectors = vectors + [ubs[:, b * width : (b + 1) * width] for b in range(hidden // width)]
    vec = jnp.concatenate(vectors + [jnp.zeros((16 - len(vectors), width), F32)], 0).astype(BF)
    for pos in range(n):
        refs, at, _d = slot(pos)
        refs[1][at, base : base + 16, :] = vec
    stores[5].start()
    stores[6].start()
    for store in stores:
        store.wait()


def solution(mesh):
    n = mesh.shape["samp"]
    groups = mesh.shape["grp"]
    gbits = groups.bit_length() - 1
    tie = lax.optimization_barrier
    swap_core = [(d, d ^ 1) for d in range(n)]
    swap_y = [(d, d ^ 2) for d in range(n)]
    same_core = [[2 * k + c for k in range(n // 2)] for c in (0, 1)]

    def swap_grp(v, bit=0):
        return lax.ppermute(v, "grp", [(d, d ^ (1 << bit)) for d in range(groups)])

    def rest_of_grp(v):
        for bit in range(1, gbits):
            v = (v.astype(F32) + swap_grp(v, bit).astype(F32)).astype(BF)
        return v

    def body(
        tokens,
        segments,
        cotangent,
        first_gain,
        first_shift,
        sample_qkv,
        sample_out,
        second_gain,
        second_shift,
        feature_qkv,
        feature_out,
        third_gain,
        third_shift,
        up_weight,
        up_bias,
        down_weight,
        down_bias,
    ):
        count, feats, width = tokens.shape[1:]
        hidden = up_weight.shape[1]
        rows = count * feats
        hpd = n // feats
        hl = H // hpd
        cl = hl * HD
        total = n * count
        heads8 = 8
        me = lax.axis_index("samp")
        r = lax.rem(me, hpd)
        x = lax.rem(lax.axis_index("grp"), 2)
        y, z = (me >> 1) & 1, me >> 2
        r1, me1, x1, y1, z1 = (v.reshape(1).astype(jnp.int32) for v in (r, me, x, y, z))
        peers = [[q + hpd * k for k in range(feats)] for q in range(hpd)]
        g1, b1, g2, b2, g3, b3, ub, db = (
            v.reshape(1, -1)
            for v in (
                first_gain,
                first_shift,
                second_gain,
                second_shift,
                third_gain,
                third_shift,
                up_bias,
                down_bias,
            )
        )

        def shift(s):
            return [(d, d // hpd * hpd + (d % hpd + s) % hpd) for d in range(n)]

        (xt,) = call(
            pack_kernel,
            [((feats, count + PAD, width), BF)],
            [pltpu.VMEM((width // LANES, rows, LANES), F32)],
            tokens[0],
            segments,
        )
        mine = lax.all_to_all(xt, "samp", 0, 0, tiled=True, axis_index_groups=peers)
        xparts = [mine] + [lax.ppermute(mine, "samp", shift(s)) for s in range(1, hpd)]

        o_send, xs, ot, lse, rank_row, rank_col, starts = call(
            functools.partial(fwd_kernel, hpd, hl),
            [
                ((n, count, cl), BF),
                ((total, width), BF),
                ((cl, total), BF),
                ((heads8, total), F32),
                ((8, total), F32),
                ((total, LANES), F32),
                ((8,), jnp.int32),
            ],
            [
                pltpu.VMEM((total, width), BF),
                pltpu.VMEM((total, LANES), F32),
                pltpu.VMEM((hl, LANES, total), BF),
                pltpu.VMEM((total, cl), BF),
                pltpu.VMEM((hl, HD + 16, total), BF),
                pltpu.VMEM((total, cl), BF),
                pltpu.VMEM((total, LANES), F32),
                pltpu.VMEM((8, total), F32),
                pltpu.VMEM((hl, HD + 16, TQ), F32),
                pltpu.VMEM((hl, 8, TQ), F32),
                pltpu.VMEM((hl, total, TQ), F32),
                pltpu.VMEM((cl, width), BF),
                pltpu.VMEM((cl, width), BF),
            ],
            r1,
            *xparts,
            g1,
            b1,
            sample_qkv,
            smem=(0,),
            smem_out=(6,),
            vmem=28,
        )
        o_recv = lax.all_to_all(o_send, "samp", 0, 0, tiled=True)

        piece = width // n
        fpiece = hidden // n
        apieces = fpiece + piece * (hidden // width)
        bpieces = piece * 5 + 16
        vm = pltpu.VMEM
        out, dx1, do_send, a_keep, a_send, b_keep, b_send = call(
            functools.partial(rows_kernel, hpd),
            [
                ((count, feats, width), BF),
                ((rows, width), F32),
                ((n, count, cl), BF),
                ((n // 2, apieces, width), BF),
                ((n // 2, apieces, width), BF),
                ((n // 2, bpieces, width), BF),
                ((n // 2, bpieces, width), BF),
            ],
            [
                vm((width, width), BF),
                vm((width, 3 * width), BF),
                vm((width, width), BF),
                vm((width, hidden), BF),
                vm((hidden, width), BF),
                vm((count, feats, width), BF),
                vm((count, feats, width), BF),
                vm((rows, width), F32),
                vm((n, count, cl), BF),
                vm((n // 2, apieces, width), BF),
                vm((n // 2, apieces, width), BF),
                vm((n // 2, bpieces, width), BF),
                vm((n // 2, bpieces, width), BF),
                vm((width // LANES, rows, LANES), F32),
                vm((rows, width), BF),
                vm((rows, width), BF),
                vm((rows, width), F32),
                vm((rows, width), BF),
                vm((feats, count, 3 * width), BF),
                vm((feats, count, width), BF),
                vm((rows, width), F32),
                vm((rows, width), BF),
                vm((rows, hidden), BF),
                vm((rows, hidden), BF),
                vm((rows, width), F32),
                vm((feats, count, width), BF),
                vm((feats, count, 3 * width), BF),
                vm((count // 16, H // 2, 32 * feats, 16 * feats), BF),
                vm((width, rows), BF),
                vm((width, width), BF),
                vm((8, hidden), F32),
                vm((hidden, width), BF),
                pltpu.SemaphoreType.DMA((6,)),
                pltpu.SemaphoreType.DMA((7,)),
            ],
            me1,
            o_recv,
            xt,
            cotangent[0],
            g2,
            b2,
            g3,
            b3,
            ub,
            db,
            sample_out,
            feature_qkv,
            feature_out,
            up_weight,
            down_weight,
            smem=(0,),
            hbm=(3, 10, 11, 12, 13, 14),
            hbm_out=tuple(range(7)),
            vmem=48,
        )
        a_got = lax.ppermute(a_send, "samp", swap_core)
        b_got = lax.ppermute(b_send, "samp", swap_core)
        do_recv = lax.all_to_all(do_send, "samp", 0, 0, tiled=True)

        qr = q_rows(cl, width)
        half = apieces // 2
        zs = n // 4

        def along_z(pieces, unit):
            return [pieces[0]] + [
                lax.ppermute(pieces[c], "samp", [(d, d ^ (unit * c)) for d in range(n)])
                for c in range(1, len(pieces))
            ]

        am, ao, cm, co = call(
            first_sums,
            [((n // 2, half, width), BF)] * 2 + [((n // 4, bpieces, width), BF)] * 2,
            [],
            x1,
            y1,
            a_keep,
            a_got,
            b_keep,
            b_got,
            smem=(0, 1),
            vmem=16,
        )
        ag, cg = swap_grp(ao), lax.ppermute(co, "samp", swap_y)
        xs_after, _ = tie((xs, am))
        k_all, v_all, kt_all, qtz, nt = call(
            functools.partial(prep_kernel, hl),
            [
                ((total, cl), BF),
                ((total, cl), BF),
                ((cl, total), BF),
                ((hl, LANES, total), BF),
                ((width, total), BF),
            ],
            [vm((cl, width), BF), vm((cl, width), BF)],
            r1,
            xs_after,
            g1,
            b1,
            sample_qkv,
            smem=(0,),
            vmem=16,
        )
        (dt,) = call(
            functools.partial(bwd_kernel, hpd, hl),
            [((3 * cl, total), BF)],
            [
                vm((total, cl), BF),
                vm((hl, LANES, total), BF),
                vm((8, total), F32),
                vm((total, LANES), F32),
                vm((8, total), F32),
                vm((cl, total), F32),
                vm((cl, total), F32),
                vm((cl, total), F32),
                vm((hl, KB, QB), BF),
                vm((hl, KB, QB), BF),
                pltpu.SMEM(((total // KB) * (total // QB),), jnp.int32),
            ],
            r1,
            starts,
            do_recv,
            k_all,
            v_all,
            kt_all,
            qtz,
            ot,
            lse,
            rank_row,
            smem=(0, 1),
            vmem=58,
        )
        am, ag, cm, cg, _ = tie((am, ag, cm, cg, dt))
        q_keep, q_send, am, ao, cm, co = call(
            dw_kernel,
            [((feats, qr, width), BF)] * 2
            + [((n // 4, half, width), BF)] * 2
            + [((zs // 2, bpieces, width), BF)] * 2,
            [vm((width, 3 * cl), F32), vm((width, 3 * cl), BF)],
            r1,
            x1,
            y1,
            z1,
            dt,
            nt,
            sample_qkv,
            g1,
            b1,
            am,
            ag,
            cm,
            cg,
            smem=(0, 1, 2, 3),
            vmem=16,
        )
        ag = lax.ppermute(ao, "samp", swap_y)
        cg = lax.ppermute(co, "samp", [(d, d ^ (n // 2)) for d in range(n)])
        dt, _ = tie((dt, q_send))
        dhs = call(
            functools.partial(dh_kernel, hpd),
            [((feats // CUTS, count, width), BF)] * (CUTS * hpd),
            [vm((width, total), BF)],
            r1,
            dt,
            sample_qkv,
            rank_col,
            smem=(0,),
            vmem=16,
        )
        parts = list(dhs[:CUTS])
        for s in range(1, hpd):
            parts += [lax.ppermute(v, "samp", shift(-s)) for v in dhs[CUTS * s : CUTS * s + CUTS]]
        pieces = call(
            middle_sums,
            [((half, width), BF)] * zs + [((bpieces, width), BF)] * (zs // 2),
            [],
            z1,
            am,
            ag,
            cm,
            cg,
            smem=(0,),
        )
        parts[0], _ = tie((parts[0], pieces[0]))
        a_pieces, c_pieces = along_z(pieces[:zs], 4), along_z(pieces[zs:], 4)
        (both,) = call(
            functools.partial(norm_kernel, hpd),
            [((feats, count + qr, width), BF)],
            [],
            *parts,
            mine,
            g1,
            q_keep,
            swap_grp(q_send),
            vmem=10,
        )
        both_send, *ends = tie((both, *a_pieces, *c_pieces))
        a_pieces, c_pieces = ends[:zs], ends[zs:]
        both = lax.all_to_all(both_send, "samp", 0, 0, tiled=True, axis_index_groups=peers)

        def last_steps(*pieces):
            (c_sum,) = call(sum_kernel, [((bpieces, width), BF)], [], *pieces[zs:])
            c_sum = rest_of_grp(c_sum)
            (a_side,) = call(sum_kernel, [((half, width), BF)], [], *pieces[:zs])
            a_side = rest_of_grp(a_side)
            return a_side, swap_grp(a_side), c_sum, swap_grp(c_sum)

        terms = (*a_pieces, *c_pieces)
        parts_summed = last_steps(*tie((*terms, both_send))[: len(terms)])
        grad_tokens, q_sum = call(
            final_kernel,
            [((count, feats, width), F32), ((qr, width), BF)],
            [vm((width // LANES, rows, LANES), F32)],
            dx1,
            both,
            vmem=12,
        )
        q_sum = rest_of_grp(q_sum)

        def from_peer(s, other):
            if not s and not other:
                return q_sum
            pairs = [
                (g * n + d, (g ^ other) * n + e) for g in range(groups) for d, e in shift(s)
            ]
            return lax.ppermute(q_sum, ("grp", "samp"), pairs)

        peers_same = [from_peer(s, 0) for s in range(hpd)]
        peers_other = [from_peer(s, 1) for s in range(hpd)]
        grad_sample_qkv, vec_sum, grad_down, grad_up, grad_fqkv, grad_fout, grad_sout, vu = call(
            functools.partial(gather_kernel, hpd),
            [
                ((piece, 3 * width), F32),
                ((8, width), F32),
                ((fpiece, width), F32),
                ((piece, hidden), F32),
                ((piece, 3 * width), F32),
                ((piece, width), F32),
                ((piece, width), F32),
                ((16, width), F32),
            ],
            [],
            r1,
            x1,
            *peers_same,
            *peers_other,
            *parts_summed,
            smem=(0, 1),
        )

        def own(v):
            return lax.dynamic_slice_in_dim(v, me * (v.shape[0] // n), v.shape[0] // n, 0)

        def own_rows(v):
            return lax.dynamic_slice_in_dim(v, me * piece, piece, 1)

        five = own_rows(vu[:5])
        two = own_rows(vec_sum[:2])
        vectors = [five[i] for i in range(5)]
        vectors.append(own(vu[5 : 5 + hidden // width].reshape(-1)))
        return (
            out[None],
            grad_tokens[None],
            two[0],
            two[1],
            grad_sample_qkv,
            grad_sout,
            vectors[0],
            vectors[1],
            grad_fqkv,
            grad_fout,
            vectors[2],
            vectors[3],
            grad_up,
            vectors[5],
            grad_down,
            vectors[4],
        )

    rep = P()
    data = P("grp", "samp", None, None)
    line = P("samp")
    flat = P("samp", None)
    in_specs = (data, P("grp", "samp"), data) + (rep,) * 14
    out_specs = (
        data,
        data,
        line,
        line,
        flat,
        flat,
        line,
        line,
        flat,
        flat,
        line,
        line,
        flat,
        line,
        flat,
        line,
    )
    return jax.shard_map(body, mesh=mesh, in_specs=in_specs, out_specs=out_specs, check_vma=False)
```

profile of v0, /device:TPU:0, one launch (start us, length us, event | category | flops | bytes accessed | tf_op | source)
XLA Modules:
  0.0 250.9 jit_solution(2021774404491388332)
XLA Ops:
  2.9 29.4 %all_to_all.20.refs_0_.refs_8_ = bf16[8,104,512]{2,1,0:T(8,128)(2,1)S(1)} all-to-all(bf16[8,104,512]{2,1,0:T(8,128)(2,1)S(1)} %shard_map.288.xt), channel_id=1, replica_groups={{0,2,4,6,8,10,12,14},{1,3,5,7,9,11,13,15},{16,18,20,22,24,26,28,30},{17..., dimensions={0} | all-to-all | bytes 1703936 | tf_op jit(solution)/shard_map/all_to_all | solution.py:1034
  32.3 2.5 collective-permute-done.refs_1_
  34.8 19.8 %shard_map.289 = (bf16[16,96,256]{2,1,0:T(8,128)(2,1)S(1)}, bf16[1536,512]{1,0:T(8,128)(2,1)S(1)}, bf16[256,1536]{1,0:T(8,128)(2,1)S(1)}, f32[8,1536]{1,0:T(8,12...) custom-call(s32[1]{0:T(128)} %bitcast.1.r_ref, ...), custom_call_target="tpu_custom_call" | custom-call | tf_op jit(solution)/shard_map/pallas_call | solution.py:98
  57.1 23.4 %all_to_all.21.o_recv = bf16[16,96,256]{2,1,0:T(8,128)(2,1)S(1)} all-to-all(bf16[16,96,256]{2,1,0:T(8,128)(2,1)S(1)} %get-tuple-element.89), channel_id=1, replica_groups=mesh['grp'=2,'samp'=16] {'samp'}, dimensions={0} | all-to-all | bytes 1572864 | tf_op jit(solution)/shard_map/all_to_all | solution.py:1072
  80.6 33.7 %shard_map.290 = (bf16[96,8,512]{2,1,0:T(8,128)(2,1)}, f32[768,512]{1,0:T(8,128)}, bf16[16,96,256]{2,1,0:T(8,128)(2,1)S(1)}, bf16[8,256,512]{2,1,0:T(8,128)(2,1)...) custom-call(s32[1]{0:T(128)} %bitcast.me_ref, ...), custom_call_target="tpu_custom_call" | custom-call | tf_op jit(solution)/shard_map/pallas_call | solution.py:98
  117.1 4.3 %all-to-all-start.2 = ((bf16[16,96,256]{2,1,0:T(8,128)(2,1)}), bf16[16,96,256]{2,1,0:T(8,128)(2,1)}, u32[]{:S(2)}, u32[]{:S(2)}) async-start(bf16[16,96,256]{2,1,0:T(8,128)(2,1)} %copy-done.20), calls=%async_computation.2 | async-start | bytes 1572864 | tf_op jit(solution)/shard_map/all_to_all | solution.py:1148
  121.4 1.9 collective-permute-done.2.c_got
  123.3 1.6 copy-done.4
  126.3 4.1 %shard_map.291 = (bf16[8,128,512]{2,1,0:T(8,128)(2,1)S(1)}, bf16[8,128,512]{2,1,0:T(8,128)(2,1)}, bf16[4,176,512]{2,1,0:T(8,128)(2,1)S(1)}, bf16[4,176,512]{2,1,0:T(8,128)(2,1)}) custom-call(s32[1]{0:T(128)} %bitcast.13.x_ref, s32[1]{0:T(128)} %bitcast.14.y_ref, bf16[8,256,512]{2,1,0:T(8,128)(2,1)S(1)} %copy-done.4, ...), custom_call_target="tpu_custom_call" | custom-call | tf_op jit(solution)/shard_map/pallas_call | solution.py:98
  135.0 3.3 %shard_map.292 = (bf16[1536,256]{1,0:T(8,128)(2,1)S(1)}, bf16[1536,256]{1,0:T(8,128)(2,1)S(1)}, bf16[256,1536]{1,0:T(8,128)(2,1)S(1)}, bf16[4,128,1536]{2,1,0:T(8,128)(2,1)S(1)}, bf16[512,1536]{1,0:T(8,128)(2,1)S(1)}) custom-call(s32[1]{0:T(128)} %bitcast.1.r_ref, bf16[1536,512]{1,0:T(8,128)(2,1)S(1)} %copy-done.9, f32[1,512]{1,0:T(1,128)S(1)} %bitcast.37, ...), custom_call_target="tpu_custom_call" | custom-call | tf_op jit(solution)/shard_map/pallas_call | solution.py:98
  143.4 18.6 %shard_map.293.dt = bf16[768,1536]{1,0:T(8,128)(2,1)} custom-call(s32[1]{0:T(128)} %bitcast.1.r_ref, s32[8]{0:T(128)} %copy-done.37, bf16[16,96,256]{2,1,0:T(8,128)(2,1)} %all-to-all-done.2.do_recv, bf16[1536,256]{1,0:T(8,128)(2,1)} %copy-done.16, bf16[1536,256]{1,0:T(8,128)(2,1)} %copy-done.17, bf16[256,1536]{1,0:T(8,128)(2,1)} %copy-done.18, ...), custom_call_target="tpu_custom_call" | custom-call | tf_op jit(solution)/shard_map/pallas_call | solution.py:98
  162.0 1.7 copy-done.1
  164.8 4.5 %shard_map.294 = (bf16[8,64,512]{2,1,0:T(8,128)(2,1)S(1)}, bf16[8,64,512]{2,1,0:T(8,128)(2,1)S(1)}, bf16[4,128,512]{2,1,0:T(8,128)(2,1)S(1)}, bf16[4,128,512]{2,...) custom-call(s32[1]{0:T(128)} %bitcast.1.r_ref, s32[1]{0:T(128)} %bitcast.13.x_ref, ...), custom_call_target="tpu_custom_call" | custom-call | tf_op jit(solution)/shard_map/pallas_call | solution.py:98
  170.6 1.6 collective-permute-start.6
  172.8 3.8 %shard_map.295 = (bf16[2,96,512]{2,1,0:T(8,128)(2,1)S(1)}, bf16[2,96,512]{2,1,0:T(8,128)(2,1)S(1)}, bf16[2,96,512]{2,1,0:T(8,128)(2,1)S(1)}, bf16[2,96,512]{2,1,...) custom-call(s32[1]{0:T(128)} %bitcast.1.r_ref, ...), custom_call_target="tpu_custom_call" | custom-call | tf_op jit(solution)/shard_map/pallas_call | solution.py:98
  177.2 12.0 %collective-permute-done.6.c_got = bf16[2,176,512]{2,1,0:T(8,128)(2,1)S(1)} collective-permute-done((bf16[2,176,512]{2,1,0:T(8,128)(2,1)S(1)}, bf16[2,176,512]{2,1,0:T(8,128)(2,1)S(1)}, u32[]{:S(2)}, u32[]{:S(2)}) %collective-permute-start.6) | collective-permute-done | bytes 360480 | tf_op jit(solution)/shard_map/ppermute | solution.py:1246
  190.0 2.0 collective-permute-start.12
  192.3 2.1 collective-permute-start.14
  196.8 5.8 %collective-permute-done.12.refs_1_ = bf16[128,512]{1,0:T(8,128)(2,1)S(1)} collective-permute-done((bf16[128,512]{1,0:T(8,128)(2,1)S(1)}, bf16[128,512]{1,0:T(8,128)(2,1)S(1)}, u32[]{:S(2)}, u32[]{:S(2)}) %collective-permute-start.12) | collective-permute-done | bytes 131104 | tf_op jit(solution)/shard_map/ppermute | solution.py:1156
  202.6 2.2 collective-permute-done.14.refs_3_
  204.9 4.1 %all-to-all-start.3 = ((bf16[8,160,512]{2,1,0:T(8,128)(2,1)}), bf16[8,160,512]{2,1,0:T(8,128)(2,1)S(1)}, u32[]{:S(2)}, u32[]{:S(2)}) async-start(bf16[8,160,512]{2,1,0:T(8,128)(2,1)} %copy-done.3), calls=%async_computation.3 | async-start | bytes 2621440 | tf_op jit(solution)/shard_map/all_to_all | solution.py:1288
  211.3 28.5 %all-to-all-done.3.both = bf16[8,160,512]{2,1,0:T(8,128)(2,1)S(1)} async-done(((bf16[8,160,512]{2,1,0:T(8,128)(2,1)}), bf16[8,160,512]{2,1,0:T(8,128)(2,1)S(1)}, u32[]{:S(2)}, u32[]{:S(2)}) %all-to-all-start.3) | async-done | bytes 1310752 | tf_op jit(solution)/shard_map/all_to_all | solution.py:1288
  241.2 1.9 shard_map.298
  245.0 3.0 %collective-permute-done.17.refs_2_ = bf16[64,512]{1,0:T(8,128)(2,1)S(1)} collective-permute-done((bf16[64,512]{1,0:T(8,128)(2,1)S(1)}, bf16[64,512]{1,0:T(8,128)(2,1)S(1)}, u32[]{:S(2)}, u32[]{:S(2)}) %collective-permute-start.17) | collective-permute-done | bytes 65568 | tf_op jit(solution)/shard_map/ppermute | solution.py:1315
  (122 shorter events, 33.9 us)
Async XLA Ops:
  32.3 2.5 %collective-permute-start = (bf16[8,104,512]{2,1,0:T(8,128)(2,1)S(1)}, bf16[8,104,512]{2,1,0:T(8,128)(2,1)}, u32[]{:S(2)}, u32[]{:S(2)}) collective-permute-start(bf16[8,104,512]{2,1,0:T(8,128)(2,1)S(1)} %all_to_all.20.refs_0_.refs_8_), channel_id=1, source_target_pairs={{0,1},{1,0},{2,3},{3,2},{4,5},{5,4},{6,7},{7,6},{8,9},{9,8},{10,11... | collective-permute-start | bytes 2555912 | tf_op jit(solution)/shard_map/ppermute | solution.py:1035
  34.8 45.7 %copy-start.25 = (bf16[512,512]{1,0:T(8,128)(2,1)S(1)}, bf16[512,512]{1,0:T(8,128)(2,1)}, u32[]{:S(2)}) copy-start(bf16[512,512]{1,0:T(8,128)(2,1)} %wfo_hbm.1) | copy-start | bytes 1572868
  116.3 7.0 %collective-permute-start.1 = (bf16[8,256,512]{2,1,0:T(8,128)(2,1)}, bf16[8,256,512]{2,1,0:T(8,128)(2,1)}, u32[]{:S(2)}, u32[]{:S(2)}) collective-permute-start(bf16[8,256,512]{2,1,0:T(8,128)(2,1)} %get-tuple-element.96), channel_id=1, source_target_pairs={{0,1},{1,0},{2,3},{3,2},{4,5},{5,4},{6,7},{7,6},{8,9},{9,8},{10,11... | collective-permute-start | bytes 6291464 | tf_op jit(solution)/shard_map/ppermute | solution.py:1146
  117.1 6.2 %collective-permute-start.2 = (bf16[8,176,512]{2,1,0:T(8,128)(2,1)}, bf16[8,176,512]{2,1,0:T(8,128)(2,1)}, u32[]{:S(2)}, u32[]{:S(2)}) collective-permute-start(bf16[8,176,512]{2,1,0:T(8,128)(2,1)} %get-tuple-element.98), channel_id=1, source_target_pairs={{0,1},{1,0},{2,3},{3,2},{4,5},{5,4},{6,7},{7,6},{8,9},{9,8},{10,11... | collective-permute-start | bytes 4325384 | tf_op jit(solution)/shard_map/ppermute | solution.py:1147
  117.1 26.2 %all-to-all-start.2 = ((bf16[16,96,256]{2,1,0:T(8,128)(2,1)}), bf16[16,96,256]{2,1,0:T(8,128)(2,1)}, u32[]{:S(2)}, u32[]{:S(2)}) async-start(bf16[16,96,256]{2,1,0:T(8,128)(2,1)} %copy-done.20), calls=%async_computation.2 | async-start | bytes 1572864 | tf_op jit(solution)/shard_map/all_to_all | solution.py:1148
  131.3 30.7 %collective-permute-start.3 = (bf16[8,128,512]{2,1,0:T(8,128)(2,1)}, bf16[8,128,512]{2,1,0:T(8,128)(2,1)}, u32[]{:S(2)}, u32[]{:S(2)}) collective-permute-start(bf16[8,128,512]{2,1,0:T(8,128)(2,1)} %get-tuple-element.109), channel_id=1, source_target_pairs={{0,16},{16,0},{1,17},{17,1},{2,18},{18,2},{3,19},{19,3},{4,20},{20... | collective-permute-start | bytes 3145736 | tf_op jit(solution)/shard_map/ppermute | solution.py:970
  132.8 29.2 %collective-permute-start.4 = (bf16[4,176,512]{2,1,0:T(8,128)(2,1)}, bf16[4,176,512]{2,1,0:T(8,128)(2,1)}, u32[]{:S(2)}, u32[]{:S(2)}) collective-permute-start(bf16[4,176,512]{2,1,0:T(8,128)(2,1)} %get-tuple-element.111), channel_id=1, source_target_pairs={{0,2},{1,3},{2,0},{3,1},{4,6},{5,7},{6,4},{7,5},{8,10},{9,11},{10,... | collective-permute-start | bytes 2162696 | tf_op jit(solution)/shard_map/ppermute | solution.py:1173
  169.3 19.8 %collective-permute-start.5 = (bf16[4,128,512]{2,1,0:T(8,128)(2,1)S(1)}, bf16[4,128,512]{2,1,0:T(8,128)(2,1)S(1)}, u32[]{:S(2)}, u32[]{:S(2)}) collective-permute-start(bf16[4,128,512]{2,1,0:T(8,128)(2,1)S(1)} %get-tuple-element.121), channel_id=1, source_target_pairs={{0,2},{1,3},{2,0},{3,1},{4,6},{5,7},{6,4},{7,5},{8,10},{9,11},{10,... | collective-permute-start | bytes 1572872 | tf_op jit(solution)/shard_map/ppermute | solution.py:1245
  170.6 18.5 %collective-permute-start.6 = (bf16[2,176,512]{2,1,0:T(8,128)(2,1)S(1)}, bf16[2,176,512]{2,1,0:T(8,128)(2,1)S(1)}, u32[]{:S(2)}, u32[]{:S(2)}) collective-permute-start(bf16[2,176,512]{2,1,0:T(8,128)(2,1)S(1)} %get-tuple-element.123), channel_id=1, source_target_pairs={{0,8},{1,9},{2,10},{3,11},{4,12},{5,13},{6,14},{7,15},{8,0},{9,1},... | collective-permute-start | bytes 1081352 | tf_op jit(solution)/shard_map/ppermute | solution.py:1246
  172.3 22.2 %collective-permute-start.11 = (bf16[8,64,512]{2,1,0:T(8,128)(2,1)S(1)}, bf16[8,64,512]{2,1,0:T(8,128)(2,1)S(1)}, u32[]{:S(2)}, u32[]{:S(2)}) collective-permute-start(bf16[8,64,512]{2,1,0:T(8,128)(2,1)S(1)} %get-tuple-element.116), channel_id=1, source_target_pairs={{0,16},{16,0},{1,17},{17,1},{2,18},{18,2},{3,19},{19,3},{4,20},{20... | collective-permute-start | bytes 1572872 | tf_op jit(solution)/shard_map/ppermute | solution.py:970
  176.6 13.3 %collective-permute-start.7 = (bf16[2,96,512]{2,1,0:T(8,128)(2,1)S(1)}, bf16[2,96,512]{2,1,0:T(8,128)(2,1)S(1)}, u32[]{:S(2)}, u32[]{:S(2)}) collective-permute-start(bf16[2,96,512]{2,1,0:T(8,128)(2,1)S(1)} %get-tuple-element.129), channel_id=1, source_target_pairs={{0,1},{1,0},{2,3},{3,2},{4,5},{5,4},{6,7},{7,6},{8,9},{9,8},{10,11... | collective-permute-start | bytes 589832 | tf_op jit(solution)/shard_map/ppermute | solution.py:1261
  176.7 13.3 %collective-permute-start.8 = (bf16[2,96,512]{2,1,0:T(8,128)(2,1)S(1)}, bf16[2,96,512]{2,1,0:T(8,128)(2,1)S(1)}, u32[]{:S(2)}, u32[]{:S(2)}) collective-permute-start(bf16[2,96,512]{2,1,0:T(8,128)(2,1)S(1)} %get-tuple-element.130), channel_id=1, source_target_pairs={{0,1},{1,0},{2,3},{3,2},{4,5},{5,4},{6,7},{7,6},{8,9},{9,8},{10,11... | collective-permute-start | bytes 589832 | tf_op jit(solution)/shard_map/ppermute | solution.py:1261
  189.2 2.8 %collective-permute-start.9 = (bf16[2,96,512]{2,1,0:T(8,128)(2,1)S(1)}, bf16[2,96,512]{2,1,0:T(8,128)(2,1)S(1)}, u32[]{:S(2)}, u32[]{:S(2)}) collective-permute-start(bf16[2,96,512]{2,1,0:T(8,128)(2,1)S(1)} %get-tuple-element.131), channel_id=1, source_target_pairs={{0,1},{1,0},{2,3},{3,2},{4,5},{5,4},{6,7},{7,6},{8,9},{9,8},{10,11... | collective-permute-start | bytes 589832 | tf_op jit(solution)/shard_map/ppermute | solution.py:1261
  189.2 3.1 %collective-permute-start.10 = (bf16[2,96,512]{2,1,0:T(8,128)(2,1)S(1)}, bf16[2,96,512]{2,1,0:T(8,128)(2,1)S(1)}, u32[]{:S(2)}, u32[]{:S(2)}) collective-permute-start(bf16[2,96,512]{2,1,0:T(8,128)(2,1)S(1)} %get-tuple-element.132), channel_id=1, source_target_pairs={{0,1},{1,0},{2,3},{3,2},{4,5},{5,4},{6,7},{7,6},{8,9},{9,8},{10,11... | collective-permute-start | bytes 589832 | tf_op jit(solution)/shard_map/ppermute | solution.py:1261
  189.9 15.0 %collective-permute-start.15 = (bf16[176,512]{1,0:T(8,128)(2,1)S(1)}, bf16[176,512]{1,0:T(8,128)(2,1)S(1)}, u32[]{:S(2)}, u32[]{:S(2)}) collective-permute-start(bf16[176,512]{1,0:T(8,128)(2,1)S(1)} %get-tuple-element.138), channel_id=1, source_target_pairs={{0,4},{1,5},{2,6},{3,7},{4,0},{5,1},{6,2},{7,3},{8,12},{9,13},{10,... | collective-permute-start | bytes 540680 | tf_op jit(solution)/shard_map/ppermute | solution.py:1156
  190.0 12.7 %collective-permute-start.12 = (bf16[128,512]{1,0:T(8,128)(2,1)S(1)}, bf16[128,512]{1,0:T(8,128)(2,1)S(1)}, u32[]{:S(2)}, u32[]{:S(2)}) collective-permute-start(bf16[128,512]{1,0:T(8,128)(2,1)S(1)} %get-tuple-element.134), channel_id=1, source_target_pairs={{0,4},{1,5},{2,6},{3,7},{4,0},{5,1},{6,2},{7,3},{8,12},{9,13},{10,... | collective-permute-start | bytes 393224 | tf_op jit(solution)/shard_map/ppermute | solution.py:1156
  192.0 10.7 %collective-permute-start.13 = (bf16[128,512]{1,0:T(8,128)(2,1)S(1)}, bf16[128,512]{1,0:T(8,128)(2,1)S(1)}, u32[]{:S(2)}, u32[]{:S(2)}) collective-permute-start(bf16[128,512]{1,0:T(8,128)(2,1)S(1)} %get-tuple-element.135), channel_id=1, source_target_pairs={{0,8},{1,9},{2,10},{3,11},{4,12},{5,13},{6,14},{7,15},{8,0},{9,1},... | collective-permute-start | bytes 393224 | tf_op jit(solution)/shard_map/ppermute | solution.py:1156
  192.3 12.6 %collective-permute-start.14 = (bf16[128,512]{1,0:T(8,128)(2,1)S(1)}, bf16[128,512]{1,0:T(8,128)(2,1)S(1)}, u32[]{:S(2)}, u32[]{:S(2)}) collective-permute-start(bf16[128,512]{1,0:T(8,128)(2,1)S(1)} %get-tuple-element.136), channel_id=1, source_target_pairs={{0,12},{1,13},{2,14},{3,15},{4,8},{5,9},{6,10},{7,11},{8,4},{9,5},... | collective-permute-start | bytes 393224 | tf_op jit(solution)/shard_map/ppermute | solution.py:1156
  204.9 34.9 %all-to-all-start.3 = ((bf16[8,160,512]{2,1,0:T(8,128)(2,1)}), bf16[8,160,512]{2,1,0:T(8,128)(2,1)S(1)}, u32[]{:S(2)}, u32[]{:S(2)}) async-start(bf16[8,160,512]{2,1,0:T(8,128)(2,1)} %copy-done.3), calls=%async_computation.3 | async-start | bytes 2621440 | tf_op jit(solution)/shard_map/all_to_all | solution.py:1288
  209.0 35.9 %collective-permute-start.20 = (bf16[176,512]{1,0:T(8,128)(2,1)S(1)}, bf16[176,512]{1,0:T(8,128)(2,1)S(1)}, u32[]{:S(2)}, u32[]{:S(2)}) collective-permute-start(bf16[176,512]{1,0:T(8,128)(2,1)S(1)} %shard_map.300.refs_6_), channel_id=1, source_target_pairs={{0,16},{16,0},{1,17},{17,1},{2,18},{18,2},{3,19},{19,3},{4,20},{20... | collective-permute-start | bytes 540680 | tf_op jit(solution)/shard_map/ppermute | solution.py:970
  209.7 35.3 %collective-permute-start.19 = (bf16[128,512]{1,0:T(8,128)(2,1)S(1)}, bf16[128,512]{1,0:T(8,128)(2,1)S(1)}, u32[]{:S(2)}, u32[]{:S(2)}) collective-permute-start(bf16[128,512]{1,0:T(8,128)(2,1)S(1)} %shard_map.299.refs_4_), channel_id=1, source_target_pairs={{0,16},{16,0},{1,17},{17,1},{2,18},{18,2},{3,19},{19,3},{4,20},{20... | collective-permute-start | bytes 393224 | tf_op jit(solution)/shard_map/ppermute | solution.py:970
  243.1 1.9 collective-permute-start.16
  243.1 4.9 %collective-permute-start.17 = (bf16[64,512]{1,0:T(8,128)(2,1)S(1)}, bf16[64,512]{1,0:T(8,128)(2,1)S(1)}, u32[]{:S(2)}, u32[]{:S(2)}) collective-permute-start(bf16[64,512]{1,0:T(8,128)(2,1)S(1)} %get-tuple-element.141.refs_0_), channel_id=1, source_target_pairs={{0,16},{1,17},{2,18},{3,19},{4,20},{5,21},{6,22},{7,23},{8,24},{9,... | collective-permute-start | bytes 196616 | tf_op jit(solution)/shard_map/ppermute | solution.py:1315
  243.6 5.0 %collective-permute-start.18 = (bf16[64,512]{1,0:T(8,128)(2,1)S(1)}, bf16[64,512]{1,0:T(8,128)(2,1)S(1)}, u32[]{:S(2)}, u32[]{:S(2)}) collective-permute-start(bf16[64,512]{1,0:T(8,128)(2,1)S(1)} %get-tuple-element.141.refs_0_), channel_id=1, source_target_pairs={{0,17},{1,16},{2,19},{3,18},{4,21},{5,20},{6,23},{7,22},{8,25},{9,... | collective-permute-start | bytes 196616 | tf_op jit(solution)/shard_map/ppermute | solution.py:1315
  (37 other events, 412.1 us)
where the time goes:
time: 252 us; the launch traced here: 251 us
  Pallas kernels  92.7 us (37%)
  waiting for transfers between devices  56.7 us (22%)
  blocking collectives  52.8 us (21%)
  starting transfers between devices  24.6 us (10%)
  local copies, waits for them, and re-layouts  23.1 us (9%)
    pallas_call x14, Pallas kernels, call(): pl.pallas_call(fn, out_shape=[jax.ShapeDtypeStruct(*o) for o in outs], in...  92.7 us
    all_to_all x1, blocking collectives, body(): mine = lax.all_to_all(xt, 'samp', 0, 0, tiled=True, axis_index_groups=peers)  29.4 us
    all_to_all x1, waiting for transfers between devices, body(): lax.all_to_all(both_send, 'samp', 0, 0, tiled=True, axis_index_groups=peers)  28.5 us
    all_to_all x1, blocking collectives, body(): o_recv = lax.all_to_all(o_send, 'samp', 0, 0, tiled=True)  23.4 us
    unnamed x78, local copies, waits for them, and re-layouts  21.9 us
    ppermute x1, waiting for transfers between devices, body(): cg = lax.ppermute(co, 'samp', [(d, d ^ n // 2) for d in range(n)])  12 us
    ppermute x4, waiting for transfers between devices, along_z(): lax.ppermute(pieces[c], 'samp', [(d, d ^ unit * c) for d in range(n)])  8.09 us
  transfers between devices with their start and end apart: 23, of which 8 were waited for; matrix products, arithmetic and copies ran while one was open for 0% of the time, Pallas kernels for 13%

commit v1 on v0

--- a/solution.py
+++ b/solution.py
@@ -403,10 +403,10 @@
     r_ref,
     start_ref,
     do_recv,
-    k_in,
-    v_in,
-    kt_in,
-    qtz,
+    k_hbm,
+    v_hbm,
+    kt_hbm,
+    qtz_hbm,
     ot,
     lse,
     rank_row,
@@ -422,7 +422,20 @@
     p_scr,
     ds_scr,
     pairs,
+    k_in,
+    v_in,
+    kt_in,
+    qtz,
+    sems,
 ):
+    loads = [
+        pltpu.make_async_copy(src, dst, sems.at[i])
+        for i, (src, dst) in enumerate(
+            ((k_hbm, k_in), (v_hbm, v_in), (kt_hbm, kt_in), (qtz_hbm, qtz))
+        )
+    ]
+    for load in loads:
+        load.start()
     feats = do_recv.shape[0] // hpd
     count = do_recv.shape[1]
     total = do_scr.shape[0]
@@ -464,6 +477,8 @@
         return lax.fori_loop(t0, t1, put, filled)
 
     filled = lax.fori_loop(0, total // KB, list_keys, jnp.int32(0))
+    for load in loads:
+        load.wait()
 
     def places(i):
         b, t = pairs[i] // 4096, lax.rem(pairs[i], 4096)
@@ -795,7 +810,7 @@
             o2[:, at, lo : lo + LANES] = jnp.transpose(ot).astype(BF).reshape(feats, part, LANES)
         return 0
 
-    lax.fori_loop(0, tiles, feat_fwd, 0, unroll=2)
+    lax.fori_loop(0, tiles, feat_fwd, 0, unroll=3)
 
     loads[3].wait()
     for b in range(2):
@@ -908,7 +923,7 @@
                 )
         return 0
 
-    lax.fori_loop(0, tiles, feat_bwd, 0, unroll=2)
+    lax.fori_loop(0, tiles, feat_bwd, 0, unroll=3)
 
     gg = jnp.zeros((1, width), F32)
     gb = jnp.zeros((1, width), F32)
@@ -1188,7 +1203,7 @@
             b1,
             sample_qkv,
             smem=(0,),
-            vmem=16,
+            vmem=58,
         )
         (dt,) = call(
             functools.partial(bwd_kernel, hpd, hl),
@@ -1205,6 +1220,11 @@
                 vm((hl, KB, QB), BF),
                 vm((hl, KB, QB), BF),
                 pltpu.SMEM(((total // KB) * (total // QB),), jnp.int32),
+                vm((total, cl), BF),
+                vm((total, cl), BF),
+                vm((cl, total), BF),
+                vm((hl, LANES, total), BF),
+                pltpu.SemaphoreType.DMA((4,)),
             ],
             r1,
             starts,
@@ -1217,6 +1237,7 @@
             lse,
             rank_row,
             smem=(0, 1),
+            hbm=(3, 4, 5, 6),
             vmem=58,
         )
         am, ag, cm, cg, _ = tie((am, ag, cm, cg, dt))

time: 252 us -> 247 us (0.980)
  local copies, waits for them, and re-layouts: 23.1 us -> 15.7 us
    unnamed x78 -> x74, local copies, waits for them, and re-layouts: 21.9 us -> 14.5 us
  transfers between devices with their start and end apart: 23 -> 23, of which waited for: 8 -> 8; matrix products, arithmetic and copies ran while one was open for 0% -> 0% of each run, Pallas kernels for 13% -> 15%
where the time goes in v1:
time: 247 us
  Pallas kernels  95 us (38%)
  waiting for transfers between devices  56.4 us (23%)
  blocking collectives  52.8 us (21%)
  starting transfers between devices  25.6 us (10%)
  local copies, waits for them, and re-layouts  15.7 us (6%)
    pallas_call x14, Pallas kernels, call(): pl.pallas_call(fn, out_shape=[jax.ShapeDtypeStruct(*o) for o in outs], in...  95 us
    all_to_all x1, blocking collectives, body(): mine = lax.all_to_all(xt, 'samp', 0, 0, tiled=True, axis_index_groups=peers)  29.4 us
    all_to_all x1, waiting for transfers between devices, body(): lax.all_to_all(both_send, 'samp', 0, 0, tiled=True, axis_index_groups=peers)  28.8 us
    all_to_all x1, blocking collectives, body(): o_recv = lax.all_to_all(o_send, 'samp', 0, 0, tiled=True)  23.4 us
    unnamed x74, local copies, waits for them, and re-layouts  14.5 us
    ppermute x1, waiting for transfers between devices, body(): cg = lax.ppermute(co, 'samp', [(d, d ^ n // 2) for d in range(n)])  10.8 us
    ppermute x4, waiting for transfers between devices, along_z(): lax.ppermute(pieces[c], 'samp', [(d, d ^ unit * c) for d in range(n)])  8.8 us
    ppermute x4, starting transfers between devices, swap_grp(): return lax.ppermute(v, 'grp', [(d, d ^ 1 << bit) for d in range(groups)])  5.16 us
  transfers between devices with their start and end apart: 23, of which 8 were waited for; matrix products, arithmetic and copies ran while one was open for 0% of the time, Pallas kernels for 15%

profile of v1, /device:TPU:0, one launch (start us, length us, event | category | flops | bytes accessed | tf_op | source)
XLA Modules:
  0.0 246.6 jit_solution(1270894636023260530)
XLA Ops:
  2.9 29.4 %all_to_all.20.refs_0_.refs_8_ = bf16[8,104,512]{2,1,0:T(8,128)(2,1)S(1)} all-to-all(bf16[8,104,512]{2,1,0:T(8,128)(2,1)S(1)} %shard_map.288.xt), channel_id=1, replica_groups={{0,2,4,6,8,10,12,14},{1,3,5,7,9,11,13,15},{16,18,20,22,24,26,28,30},{17..., dimensions={0} | all-to-all | bytes 1703936 | tf_op jit(solution)/shard_map/all_to_all | solution.py:1049
  32.3 2.5 %collective-permute-done.refs_1_ = bf16[8,104,512]{2,1,0:T(8,128)(2,1)} collective-permute-done((bf16[8,104,512]{2,1,0:T(8,128)(2,1)S(1)}, bf16[8,104,512]{2,1,0:T(8,128)(2,1)}, u32[]{:S(2)}, u32[]{:S(2)}) %collective-permute-start) | collective-permute-done | bytes 852000 | tf_op jit(solution)/shard_map/ppermute | solution.py:1050
  34.8 19.8 %shard_map.289 = (bf16[16,96,256]{2,1,0:T(8,128)(2,1)S(1)}, bf16[1536,512]{1,0:T(8,128)(2,1)S(1)}, bf16[256,1536]{1,0:T(8,128)(2,1)S(1)}, f32[8,1536]{1,0:T(8,12...) custom-call(s32[1]{0:T(128)} %bitcast.1.r_ref, ...), custom_call_target="tpu_custom_call" | custom-call | tf_op jit(solution)/shard_map/pallas_call | solution.py:98
  57.1 23.4 %all_to_all.21.o_recv = bf16[16,96,256]{2,1,0:T(8,128)(2,1)S(1)} all-to-all(bf16[16,96,256]{2,1,0:T(8,128)(2,1)S(1)} %get-tuple-element.89), channel_id=1, replica_groups=mesh['grp'=2,'samp'=16] {'samp'}, dimensions={0} | all-to-all | bytes 1572864 | tf_op jit(solution)/shard_map/all_to_all | solution.py:1087
  80.6 33.0 %shard_map.290 = (bf16[96,8,512]{2,1,0:T(8,128)(2,1)}, f32[768,512]{1,0:T(8,128)}, bf16[16,96,256]{2,1,0:T(8,128)(2,1)S(1)}, bf16[8,256,512]{2,1,0:T(8,128)(2,1)...) custom-call(s32[1]{0:T(128)} %bitcast.me_ref, ...), custom_call_target="tpu_custom_call" | custom-call | tf_op jit(solution)/shard_map/pallas_call | solution.py:98
  115.6 4.3 %all-to-all-start.2 = ((bf16[16,96,256]{2,1,0:T(8,128)(2,1)}), bf16[16,96,256]{2,1,0:T(8,128)(2,1)}, u32[]{:S(2)}, u32[]{:S(2)}) async-start(bf16[16,96,256]{2,1,0:T(8,128)(2,1)} %copy-done.16), calls=%async_computation.2 | async-start | bytes 1572864 | tf_op jit(solution)/shard_map/all_to_all | solution.py:1163
  119.9 1.7 collective-permute-done.2.c_got
  121.6 1.6 copy-done.4
  124.6 3.4 %shard_map.291 = (bf16[8,128,512]{2,1,0:T(8,128)(2,1)S(1)}, bf16[8,128,512]{2,1,0:T(8,128)(2,1)}, bf16[4,176,512]{2,1,0:T(8,128)(2,1)S(1)}, bf16[4,176,512]{2,1,0:T(8,128)(2,1)}) custom-call(s32[1]{0:T(128)} %bitcast.13.x_ref, s32[1]{0:T(128)} %bitcast.14.y_ref, bf16[8,256,512]{2,1,0:T(8,128)(2,1)S(1)} %copy-done.4, ...), custom_call_target="tpu_custom_call" | custom-call | tf_op jit(solution)/shard_map/pallas_call | solution.py:98
  132.2 7.2 %shard_map.292 = (bf16[1536,256]{1,0:T(8,128)(2,1)}, bf16[1536,256]{1,0:T(8,128)(2,1)}, bf16[256,1536]{1,0:T(8,128)(2,1)}, bf16[4,128,1536]{2,1,0:T(8,128)(2,1)}, bf16[512,1536]{1,0:T(8,128)(2,1)}) custom-call(s32[1]{0:T(128)} %bitcast.1.r_ref, bf16[1536,512]{1,0:T(8,128)(2,1)} %copy-done.7, f32[1,512]{1,0:T(1,128)} %bitcast.36, f32[1,512]{1,0:T(1,128)} %bitcast.40, ...), custom_call_target="tpu_custom_call" | custom-call | tf_op jit(solution)/shard_map/pallas_call | solution.py:98
  139.5 17.4 %shard_map.293.dt = bf16[768,1536]{1,0:T(8,128)(2,1)} custom-call(s32[1]{0:T(128)} %bitcast.1.r_ref, s32[8]{0:T(128)} %copy-done.35, bf16[16,96,256]{2,1,0:T(8,128)(2,1)} %all-to-all-done.2.do_recv, bf16[1536,256]{1,0:T(8,128)(2,1)} %get-tuple-element.101.k_hbm, bf16[1536,256]{1,0:T(8,128)(2,1)} %get-tuple-element.102.v_hbm, ...), custom_call_target="tpu_custom_call" | custom-call | tf_op jit(solution)/shard_map/pallas_call | solution.py:98
  157.0 1.7 copy-done.2
  159.8 4.2 %shard_map.294 = (bf16[8,64,512]{2,1,0:T(8,128)(2,1)S(1)}, bf16[8,64,512]{2,1,0:T(8,128)(2,1)S(1)}, bf16[4,128,512]{2,1,0:T(8,128)(2,1)S(1)}, bf16[4,128,512]{2,...) custom-call(s32[1]{0:T(128)} %bitcast.1.r_ref, s32[1]{0:T(128)} %bitcast.13.x_ref, ...), custom_call_target="tpu_custom_call" | custom-call | tf_op jit(solution)/shard_map/pallas_call | solution.py:98
  165.3 1.8 collective-permute-start.6
  168.6 3.8 %shard_map.295 = (bf16[2,96,512]{2,1,0:T(8,128)(2,1)S(1)}, bf16[2,96,512]{2,1,0:T(8,128)(2,1)S(1)}, bf16[2,96,512]{2,1,0:T(8,128)(2,1)S(1)}, bf16[2,96,512]{2,1,...) custom-call(s32[1]{0:T(128)} %bitcast.1.r_ref, ...), custom_call_target="tpu_custom_call" | custom-call | tf_op jit(solution)/shard_map/pallas_call | solution.py:98
  173.0 10.8 %collective-permute-done.6.c_got = bf16[2,176,512]{2,1,0:T(8,128)(2,1)S(1)} collective-permute-done((bf16[2,176,512]{2,1,0:T(8,128)(2,1)S(1)}, bf16[2,176,512]{2,1,0:T(8,128)(2,1)S(1)}, u32[]{:S(2)}, u32[]{:S(2)}) %collective-permute-start.6) | collective-permute-done | bytes 360480 | tf_op jit(solution)/shard_map/ppermute | solution.py:1267
  184.6 2.0 collective-permute-start.12
  189.4 2.4 shard_map.297
  191.8 4.9 %collective-permute-done.12.refs_1_ = bf16[128,512]{1,0:T(8,128)(2,1)S(1)} collective-permute-done((bf16[128,512]{1,0:T(8,128)(2,1)S(1)}, bf16[128,512]{1,0:T(8,128)(2,1)S(1)}, u32[]{:S(2)}, u32[]{:S(2)}) %collective-permute-start.12) | collective-permute-done | bytes 131104 | tf_op jit(solution)/shard_map/ppermute | solution.py:1171
  196.7 3.9 %collective-permute-done.14.refs_3_ = bf16[128,512]{1,0:T(8,128)(2,1)S(1)} collective-permute-done((bf16[128,512]{1,0:T(8,128)(2,1)S(1)}, bf16[128,512]{1,0:T(8,128)(2,1)S(1)}, u32[]{:S(2)}, u32[]{:S(2)}) %collective-permute-start.14) | collective-permute-done | bytes 131104 | tf_op jit(solution)/shard_map/ppermute | solution.py:1171
  200.6 3.7 %all-to-all-start.3 = ((bf16[8,160,512]{2,1,0:T(8,128)(2,1)}), bf16[8,160,512]{2,1,0:T(8,128)(2,1)S(1)}, u32[]{:S(2)}, u32[]{:S(2)}) async-start(bf16[8,160,512]{2,1,0:T(8,128)(2,1)} %shard_map.297), calls=%async_computation.3 | async-start | bytes 2621440 | tf_op jit(solution)/shard_map/all_to_all | solution.py:1309
  206.5 28.8 %all-to-all-done.3.both = bf16[8,160,512]{2,1,0:T(8,128)(2,1)S(1)} async-done(((bf16[8,160,512]{2,1,0:T(8,128)(2,1)}), bf16[8,160,512]{2,1,0:T(8,128)(2,1)S(1)}, u32[]{:S(2)}, u32[]{:S(2)}) %all-to-all-start.3) | async-done | bytes 1310752 | tf_op jit(solution)/shard_map/all_to_all | solution.py:1309
  236.8 1.9 shard_map.298
  240.5 2.7 %collective-permute-done.17.refs_2_ = bf16[64,512]{1,0:T(8,128)(2,1)S(1)} collective-permute-done((bf16[64,512]{1,0:T(8,128)(2,1)S(1)}, bf16[64,512]{1,0:T(8,128)(2,1)S(1)}, u32[]{:S(2)}, u32[]{:S(2)}) %collective-permute-start.17) | collective-permute-done | bytes 65568 | tf_op jit(solution)/shard_map/ppermute | solution.py:1336
  (118 shorter events, 29.2 us)
Async XLA Ops:
  32.3 2.5 %collective-permute-start = (bf16[8,104,512]{2,1,0:T(8,128)(2,1)S(1)}, bf16[8,104,512]{2,1,0:T(8,128)(2,1)}, u32[]{:S(2)}, u32[]{:S(2)}) collective-permute-start(bf16[8,104,512]{2,1,0:T(8,128)(2,1)S(1)} %all_to_all.20.refs_0_.refs_8_), channel_id=1, source_target_pairs={{0,1},{1,0},{2,3},{3,2},{4,5},{5,4},{6,7},{7,6},{8,9},{9,8},{10,11... | collective-permute-start | bytes 2555912 | tf_op jit(solution)/shard_map/ppermute | solution.py:1050
  34.8 45.7 %copy-start.21 = (bf16[512,512]{1,0:T(8,128)(2,1)S(1)}, bf16[512,512]{1,0:T(8,128)(2,1)}, u32[]{:S(2)}) copy-start(bf16[512,512]{1,0:T(8,128)(2,1)} %wfo_hbm.1) | copy-start | bytes 1572868
  114.7 6.9 %collective-permute-start.1 = (bf16[8,256,512]{2,1,0:T(8,128)(2,1)}, bf16[8,256,512]{2,1,0:T(8,128)(2,1)S(1)}, u32[]{:S(2)}, u32[]{:S(2)}) collective-permute-start(bf16[8,256,512]{2,1,0:T(8,128)(2,1)} %get-tuple-element.96), channel_id=1, source_target_pairs={{0,1},{1,0},{2,3},{3,2},{4,5},{5,4},{6,7},{7,6},{8,9},{9,8},{10,11... | collective-permute-start | bytes 6291464 | tf_op jit(solution)/shard_map/ppermute | solution.py:1161
  115.5 6.1 %collective-permute-start.2 = (bf16[8,176,512]{2,1,0:T(8,128)(2,1)}, bf16[8,176,512]{2,1,0:T(8,128)(2,1)}, u32[]{:S(2)}, u32[]{:S(2)}) collective-permute-start(bf16[8,176,512]{2,1,0:T(8,128)(2,1)} %get-tuple-element.98), channel_id=1, source_target_pairs={{0,1},{1,0},{2,3},{3,2},{4,5},{5,4},{6,7},{7,6},{8,9},{9,8},{10,11... | collective-permute-start | bytes 4325384 | tf_op jit(solution)/shard_map/ppermute | solution.py:1162
  115.6 23.8 %all-to-all-start.2 = ((bf16[16,96,256]{2,1,0:T(8,128)(2,1)}), bf16[16,96,256]{2,1,0:T(8,128)(2,1)}, u32[]{:S(2)}, u32[]{:S(2)}) async-start(bf16[16,96,256]{2,1,0:T(8,128)(2,1)} %copy-done.16), calls=%async_computation.2 | async-start | bytes 1572864 | tf_op jit(solution)/shard_map/all_to_all | solution.py:1163
  129.9 27.1 %collective-permute-start.3 = (bf16[8,128,512]{2,1,0:T(8,128)(2,1)}, bf16[8,128,512]{2,1,0:T(8,128)(2,1)S(1)}, u32[]{:S(2)}, u32[]{:S(2)}) collective-permute-start(bf16[8,128,512]{2,1,0:T(8,128)(2,1)} %get-tuple-element.109), channel_id=1, source_target_pairs={{0,16},{16,0},{1,17},{17,1},{2,18},{18,2},{3,19},{19,3},{4,20},{20... | collective-permute-start | bytes 3145736 | tf_op jit(solution)/shard_map/ppermute | solution.py:985
  131.4 25.5 %collective-permute-start.4 = (bf16[4,176,512]{2,1,0:T(8,128)(2,1)}, bf16[4,176,512]{2,1,0:T(8,128)(2,1)}, u32[]{:S(2)}, u32[]{:S(2)}) collective-permute-start(bf16[4,176,512]{2,1,0:T(8,128)(2,1)} %get-tuple-element.111), channel_id=1, source_target_pairs={{0,2},{1,3},{2,0},{3,1},{4,6},{5,7},{6,4},{7,5},{8,10},{9,11},{10,... | collective-permute-start | bytes 2162696 | tf_op jit(solution)/shard_map/ppermute | solution.py:1188
  164.0 19.8 %collective-permute-start.5 = (bf16[4,128,512]{2,1,0:T(8,128)(2,1)S(1)}, bf16[4,128,512]{2,1,0:T(8,128)(2,1)S(1)}, u32[]{:S(2)}, u32[]{:S(2)}) collective-permute-start(bf16[4,128,512]{2,1,0:T(8,128)(2,1)S(1)} %get-tuple-element.121), channel_id=1, source_target_pairs={{0,2},{1,3},{2,0},{3,1},{4,6},{5,7},{6,4},{7,5},{8,10},{9,11},{10,... | collective-permute-start | bytes 1572872 | tf_op jit(solution)/shard_map/ppermute | solution.py:1266
  165.3 18.5 %collective-permute-start.6 = (bf16[2,176,512]{2,1,0:T(8,128)(2,1)S(1)}, bf16[2,176,512]{2,1,0:T(8,128)(2,1)S(1)}, u32[]{:S(2)}, u32[]{:S(2)}) collective-permute-start(bf16[2,176,512]{2,1,0:T(8,128)(2,1)S(1)} %get-tuple-element.123), channel_id=1, source_target_pairs={{0,8},{1,9},{2,10},{3,11},{4,12},{5,13},{6,14},{7,15},{8,0},{9,1},... | collective-permute-start | bytes 1081352 | tf_op jit(solution)/shard_map/ppermute | solution.py:1267
  167.1 22.3 %collective-permute-start.11 = (bf16[8,64,512]{2,1,0:T(8,128)(2,1)S(1)}, bf16[8,64,512]{2,1,0:T(8,128)(2,1)S(1)}, u32[]{:S(2)}, u32[]{:S(2)}) collective-permute-start(bf16[8,64,512]{2,1,0:T(8,128)(2,1)S(1)} %get-tuple-element.116), channel_id=1, source_target_pairs={{0,16},{16,0},{1,17},{17,1},{2,18},{18,2},{3,19},{19,3},{4,20},{20... | collective-permute-start | bytes 1572872 | tf_op jit(solution)/shard_map/ppermute | solution.py:985
  172.4 12.1 %collective-permute-start.7 = (bf16[2,96,512]{2,1,0:T(8,128)(2,1)S(1)}, bf16[2,96,512]{2,1,0:T(8,128)(2,1)S(1)}, u32[]{:S(2)}, u32[]{:S(2)}) collective-permute-start(bf16[2,96,512]{2,1,0:T(8,128)(2,1)S(1)} %get-tuple-element.129), channel_id=1, source_target_pairs={{0,1},{1,0},{2,3},{3,2},{4,5},{5,4},{6,7},{7,6},{8,9},{9,8},{10,11... | collective-permute-start | bytes 589832 | tf_op jit(solution)/shard_map/ppermute | solution.py:1282
  172.5 12.1 %collective-permute-start.8 = (bf16[2,96,512]{2,1,0:T(8,128)(2,1)S(1)}, bf16[2,96,512]{2,1,0:T(8,128)(2,1)S(1)}, u32[]{:S(2)}, u32[]{:S(2)}) collective-permute-start(bf16[2,96,512]{2,1,0:T(8,128)(2,1)S(1)} %get-tuple-element.130), channel_id=1, source_target_pairs={{0,1},{1,0},{2,3},{3,2},{4,5},{5,4},{6,7},{7,6},{8,9},{9,8},{10,11... | collective-permute-start | bytes 589832 | tf_op jit(solution)/shard_map/ppermute | solution.py:1282
  183.8 2.8 %collective-permute-start.9 = (bf16[2,96,512]{2,1,0:T(8,128)(2,1)S(1)}, bf16[2,96,512]{2,1,0:T(8,128)(2,1)S(1)}, u32[]{:S(2)}, u32[]{:S(2)}) collective-permute-start(bf16[2,96,512]{2,1,0:T(8,128)(2,1)S(1)} %get-tuple-element.131), channel_id=1, source_target_pairs={{0,1},{1,0},{2,3},{3,2},{4,5},{5,4},{6,7},{7,6},{8,9},{9,8},{10,11... | collective-permute-start | bytes 589832 | tf_op jit(solution)/shard_map/ppermute | solution.py:1282
  183.8 4.2 %collective-permute-start.10 = (bf16[2,96,512]{2,1,0:T(8,128)(2,1)S(1)}, bf16[2,96,512]{2,1,0:T(8,128)(2,1)S(1)}, u32[]{:S(2)}, u32[]{:S(2)}) collective-permute-start(bf16[2,96,512]{2,1,0:T(8,128)(2,1)S(1)} %get-tuple-element.132), channel_id=1, source_target_pairs={{0,1},{1,0},{2,3},{3,2},{4,5},{5,4},{6,7},{7,6},{8,9},{9,8},{10,11... | collective-permute-start | bytes 589832 | tf_op jit(solution)/shard_map/ppermute | solution.py:1282
  184.5 16.0 %collective-permute-start.15 = (bf16[176,512]{1,0:T(8,128)(2,1)S(1)}, bf16[176,512]{1,0:T(8,128)(2,1)S(1)}, u32[]{:S(2)}, u32[]{:S(2)}) collective-permute-start(bf16[176,512]{1,0:T(8,128)(2,1)S(1)} %get-tuple-element.138), channel_id=1, source_target_pairs={{0,4},{1,5},{2,6},{3,7},{4,0},{5,1},{6,2},{7,3},{8,12},{9,13},{10,... | collective-permute-start | bytes 540680 | tf_op jit(solution)/shard_map/ppermute | solution.py:1171
  184.6 12.1 %collective-permute-start.12 = (bf16[128,512]{1,0:T(8,128)(2,1)S(1)}, bf16[128,512]{1,0:T(8,128)(2,1)S(1)}, u32[]{:S(2)}, u32[]{:S(2)}) collective-permute-start(bf16[128,512]{1,0:T(8,128)(2,1)S(1)} %get-tuple-element.134), channel_id=1, source_target_pairs={{0,4},{1,5},{2,6},{3,7},{4,0},{5,1},{6,2},{7,3},{8,12},{9,13},{10,... | collective-permute-start | bytes 393224 | tf_op jit(solution)/shard_map/ppermute | solution.py:1171
  186.6 10.0 %collective-permute-start.13 = (bf16[128,512]{1,0:T(8,128)(2,1)S(1)}, bf16[128,512]{1,0:T(8,128)(2,1)S(1)}, u32[]{:S(2)}, u32[]{:S(2)}) collective-permute-start(bf16[128,512]{1,0:T(8,128)(2,1)S(1)} %get-tuple-element.135), channel_id=1, source_target_pairs={{0,8},{1,9},{2,10},{3,11},{4,12},{5,13},{6,14},{7,15},{8,0},{9,1},... | collective-permute-start | bytes 393224 | tf_op jit(solution)/shard_map/ppermute | solution.py:1171
  188.0 12.6 %collective-permute-start.14 = (bf16[128,512]{1,0:T(8,128)(2,1)S(1)}, bf16[128,512]{1,0:T(8,128)(2,1)S(1)}, u32[]{:S(2)}, u32[]{:S(2)}) collective-permute-start(bf16[128,512]{1,0:T(8,128)(2,1)S(1)} %get-tuple-element.136), channel_id=1, source_target_pairs={{0,12},{1,13},{2,14},{3,15},{4,8},{5,9},{6,10},{7,11},{8,4},{9,5},... | collective-permute-start | bytes 393224 | tf_op jit(solution)/shard_map/ppermute | solution.py:1171
  200.6 34.8 %all-to-all-start.3 = ((bf16[8,160,512]{2,1,0:T(8,128)(2,1)}), bf16[8,160,512]{2,1,0:T(8,128)(2,1)S(1)}, u32[]{:S(2)}, u32[]{:S(2)}) async-start(bf16[8,160,512]{2,1,0:T(8,128)(2,1)} %shard_map.297), calls=%async_computation.3 | async-start | bytes 2621440 | tf_op jit(solution)/shard_map/all_to_all | solution.py:1309
  204.3 36.2 %collective-permute-start.20 = (bf16[176,512]{1,0:T(8,128)(2,1)S(1)}, bf16[176,512]{1,0:T(8,128)(2,1)S(1)}, u32[]{:S(2)}, u32[]{:S(2)}) collective-permute-start(bf16[176,512]{1,0:T(8,128)(2,1)S(1)} %shard_map.300.refs_6_), channel_id=1, source_target_pairs={{0,16},{16,0},{1,17},{17,1},{2,18},{18,2},{3,19},{19,3},{4,20},{20... | collective-permute-start | bytes 540680 | tf_op jit(solution)/shard_map/ppermute | solution.py:985
  205.9 34.6 %collective-permute-start.19 = (bf16[128,512]{1,0:T(8,128)(2,1)S(1)}, bf16[128,512]{1,0:T(8,128)(2,1)S(1)}, u32[]{:S(2)}, u32[]{:S(2)}) collective-permute-start(bf16[128,512]{1,0:T(8,128)(2,1)S(1)} %shard_map.299.refs_4_), channel_id=1, source_target_pairs={{0,16},{16,0},{1,17},{17,1},{2,18},{18,2},{3,19},{19,3},{4,20},{20... | collective-permute-start | bytes 393224 | tf_op jit(solution)/shard_map/ppermute | solution.py:985
  238.7 1.9 collective-permute-start.16
  238.7 4.5 %collective-permute-start.17 = (bf16[64,512]{1,0:T(8,128)(2,1)S(1)}, bf16[64,512]{1,0:T(8,128)(2,1)S(1)}, u32[]{:S(2)}, u32[]{:S(2)}) collective-permute-start(bf16[64,512]{1,0:T(8,128)(2,1)S(1)} %get-tuple-element.141.refs_0_), channel_id=1, source_target_pairs={{0,16},{1,17},{2,18},{3,19},{4,20},{5,21},{6,22},{7,23},{8,24},{9,... | collective-permute-start | bytes 196616 | tf_op jit(solution)/shard_map/ppermute | solution.py:1336
  240.2 4.1 %collective-permute-start.18 = (bf16[64,512]{1,0:T(8,128)(2,1)S(1)}, bf16[64,512]{1,0:T(8,128)(2,1)S(1)}, u32[]{:S(2)}, u32[]{:S(2)}) collective-permute-start(bf16[64,512]{1,0:T(8,128)(2,1)S(1)} %get-tuple-element.141.refs_0_), channel_id=1, source_target_pairs={{0,17},{1,16},{2,19},{3,18},{4,21},{5,20},{6,23},{7,22},{8,25},{9,... | collective-permute-start | bytes 196616 | tf_op jit(solution)/shard_map/ppermute | solution.py:1336
  (35 other events, 476.1 us)

commit v2 on v1

--- a/solution.py
+++ b/solution.py
@@ -1082,7 +1082,7 @@
             sample_qkv,
             smem=(0,),
             smem_out=(6,),
-            vmem=28,
+            vmem=58,
         )
         o_recv = lax.all_to_all(o_send, "samp", 0, 0, tiled=True)
 

time: 247 us -> 246 us (level)
  waiting for transfers between devices: 56.4 us -> 52.5 us
  Pallas kernels: 95 us -> 97.6 us
    all_to_all x1, waiting for transfers between devices: 28.8 us -> 25.6 us  [body(): lax.all_to_all(both_send, 'samp', 0, 0, tiled=True, axis_index_groups=peers)]
    pallas_call x14, Pallas kernels: 95 us -> 97.6 us  [call(): pl.pallas_call(fn, out_shape=[jax.ShapeDtypeStruct(*o) for o in outs], in...]
    unnamed x74 -> x72, local copies, waits for them, and re-layouts: 14.5 us -> 12.7 us
  transfers between devices with their start and end apart: 23 -> 23, of which waited for: 8 -> 10; matrix products, arithmetic and copies ran while one was open for 0% -> 0% of each run, Pallas kernels for 15% -> 15%
where the time goes in v2:
time: 246 us
  Pallas kernels  97.6 us (40%)
  blocking collectives  53.2 us (22%)
  waiting for transfers between devices  52.5 us (21%)
  starting transfers between devices  27.2 us (11%)
  local copies, waits for them, and re-layouts  13.9 us (6%)
    pallas_call x14, Pallas kernels, call(): pl.pallas_call(fn, out_shape=[jax.ShapeDtypeStruct(*o) for o in outs], in...  97.6 us
    all_to_all x1, blocking collectives, body(): mine = lax.all_to_all(xt, 'samp', 0, 0, tiled=True, axis_index_groups=peers)  29.3 us
    all_to_all x1, waiting for transfers between devices, body(): lax.all_to_all(both_send, 'samp', 0, 0, tiled=True, axis_index_groups=peers)  25.6 us
    all_to_all x1, blocking collectives, body(): o_recv = lax.all_to_all(o_send, 'samp', 0, 0, tiled=True)  24 us
    unnamed x72, local copies, waits for them, and re-layouts  12.7 us
    ppermute x1, waiting for transfers between devices, body(): cg = lax.ppermute(co, 'samp', [(d, d ^ n // 2) for d in range(n)])  10.7 us
    ppermute x4, waiting for transfers between devices, along_z(): lax.ppermute(pieces[c], 'samp', [(d, d ^ unit * c) for d in range(n)])  7.51 us
    ppermute x4, starting transfers between devices, swap_grp(): return lax.ppermute(v, 'grp', [(d, d ^ 1 << bit) for d in range(groups)])  5.16 us
  transfers between devices with their start and end apart: 23, of which 10 were waited for; matrix products, arithmetic and copies ran while one was open for 0% of the time, Pallas kernels for 15%

profile of v2, /device:TPU:0, one launch (start us, length us, event | category | flops | bytes accessed | tf_op | source)
XLA Modules:
  0.0 245.5 jit_solution(10704795486543313400)
XLA Ops:
  2.9 29.3 %all_to_all.20.refs_0_.refs_8_ = bf16[8,104,512]{2,1,0:T(8,128)(2,1)S(1)} all-to-all(bf16[8,104,512]{2,1,0:T(8,128)(2,1)S(1)} %shard_map.288.xt), channel_id=1, replica_groups={{0,2,4,6,8,10,12,14},{1,3,5,7,9,11,13,15},{16,18,20,22,24,26,28,30},{17..., dimensions={0} | all-to-all | bytes 1703936 | tf_op jit(solution)/shard_map/all_to_all | solution.py:1049
  32.1 2.4 collective-permute-done.refs_1_
  35.4 21.5 %shard_map.289 = (bf16[16,96,256]{2,1,0:T(8,128)(2,1)}, bf16[1536,512]{1,0:T(8,128)(2,1)}, bf16[256,1536]{1,0:T(8,128)(2,1)}, f32[8,1536]{1,0:T(8,128)}, f32[8,1...) custom-call(s32[1]{0:T(128)} %bitcast.1.r_ref, bf16[8,104,512]{2,1,0:T(8,128)(2,1)} %copy-done.3, ...), custom_call_target="tpu_custom_call" | custom-call | tf_op jit(solution)/shard_map/pallas_call | solution.py:98
  57.1 24.0 %all_to_all.21.o_recv = bf16[16,96,256]{2,1,0:T(8,128)(2,1)S(1)} all-to-all(bf16[16,96,256]{2,1,0:T(8,128)(2,1)} %get-tuple-element.89), channel_id=1, replica_groups=mesh['grp'=2,'samp'=16] {'samp'}, dimensions={0} | all-to-all | bytes 1572864 | tf_op jit(solution)/shard_map/all_to_all | solution.py:1087
  81.1 32.9 %shard_map.290 = (bf16[96,8,512]{2,1,0:T(8,128)(2,1)}, f32[768,512]{1,0:T(8,128)}, bf16[16,96,256]{2,1,0:T(8,128)(2,1)S(1)}, bf16[8,256,512]{2,1,0:T(8,128)(2,1)...) custom-call(s32[1]{0:T(128)} %bitcast.me_ref, ...), custom_call_target="tpu_custom_call" | custom-call | tf_op jit(solution)/shard_map/pallas_call | solution.py:98
  115.0 4.3 %all-to-all-start.2 = ((bf16[16,96,256]{2,1,0:T(8,128)(2,1)}), bf16[16,96,256]{2,1,0:T(8,128)(2,1)}, u32[]{:S(2)}, u32[]{:S(2)}) async-start(bf16[16,96,256]{2,1,0:T(8,128)(2,1)} %copy-done.12), calls=%async_computation.2 | async-start | bytes 1572864 | tf_op jit(solution)/shard_map/all_to_all | solution.py:1163
  119.3 1.7 collective-permute-done.2.c_got
  122.6 3.4 %shard_map.291 = (bf16[8,128,512]{2,1,0:T(8,128)(2,1)S(1)}, bf16[8,128,512]{2,1,0:T(8,128)(2,1)}, bf16[4,176,512]{2,1,0:T(8,128)(2,1)S(1)}, bf16[4,176,512]{2,1,0:T(8,128)(2,1)}) custom-call(s32[1]{0:T(128)} %bitcast.13.x_ref, s32[1]{0:T(128)} %bitcast.14.y_ref, bf16[8,256,512]{2,1,0:T(8,128)(2,1)S(1)} %copy-done.5, ...), custom_call_target="tpu_custom_call" | custom-call | tf_op jit(solution)/shard_map/pallas_call | solution.py:98
  130.2 7.3 %shard_map.292 = (bf16[1536,256]{1,0:T(8,128)(2,1)}, bf16[1536,256]{1,0:T(8,128)(2,1)}, bf16[256,1536]{1,0:T(8,128)(2,1)}, bf16[4,128,1536]{2,1,0:T(8,128)(2,1)}, bf16[512,1536]{1,0:T(8,128)(2,1)}) custom-call(s32[1]{0:T(128)} %bitcast.1.r_ref, bf16[1536,512]{1,0:T(8,128)(2,1)} %get-tuple-element.100.xs, f32[1,512]{1,0:T(1,128)} %bitcast.37, ...), custom_call_target="tpu_custom_call" | custom-call | tf_op jit(solution)/shard_map/pallas_call | solution.py:98
  138.1 17.5 %shard_map.293.dt = bf16[768,1536]{1,0:T(8,128)(2,1)} custom-call(s32[1]{0:T(128)} %bitcast.1.r_ref, s32[8]{0:T(128)} %get-tuple-element.92.start_ref, bf16[16,96,256]{2,1,0:T(8,128)(2,1)} %all-to-all-done.2.do_recv, bf16[1536,256]{1,0:T(8,128)(2,1)} %get-tuple-element.101.k_hbm, bf16[1536,256]{1,0:T(8,128)(2,1)} %get-tuple-element.102.v_hbm, ...), custom_call_target="tpu_custom_call" | custom-call | tf_op jit(solution)/shard_map/pallas_call | solution.py:98
  155.6 1.7 copy-done.1
  157.3 4.3 %shard_map.294 = (bf16[8,64,512]{2,1,0:T(8,128)(2,1)S(1)}, bf16[8,64,512]{2,1,0:T(8,128)(2,1)S(1)}, bf16[4,128,512]{2,1,0:T(8,128)(2,1)S(1)}, bf16[4,128,512]{2,...) custom-call(s32[1]{0:T(128)} %bitcast.1.r_ref, s32[1]{0:T(128)} %bitcast.13.x_ref, ...), custom_call_target="tpu_custom_call" | custom-call | tf_op jit(solution)/shard_map/pallas_call | solution.py:98
  162.8 2.7 %collective-permute-start.6 = (bf16[2,176,512]{2,1,0:T(8,128)(2,1)S(1)}, bf16[2,176,512]{2,1,0:T(8,128)(2,1)S(1)}, u32[]{:S(2)}, u32[]{:S(2)}) collective-permute-start(bf16[2,176,512]{2,1,0:T(8,128)(2,1)S(1)} %get-tuple-element.123), channel_id=1, source_target_pairs={{0,8},{1,9},{2,10},{3,11},{4,12},{5,13},{6,14},{7,15},{8,0},{9,1},... | collective-permute-start | bytes 1081352 | tf_op jit(solution)/shard_map/ppermute | solution.py:1267
  167.0 3.8 %shard_map.295 = (bf16[2,96,512]{2,1,0:T(8,128)(2,1)S(1)}, bf16[2,96,512]{2,1,0:T(8,128)(2,1)S(1)}, bf16[2,96,512]{2,1,0:T(8,128)(2,1)S(1)}, bf16[2,96,512]{2,1,...) custom-call(s32[1]{0:T(128)} %bitcast.1.r_ref, ...), custom_call_target="tpu_custom_call" | custom-call | tf_op jit(solution)/shard_map/pallas_call | solution.py:98
  171.4 10.7 %collective-permute-done.6.c_got = bf16[2,176,512]{2,1,0:T(8,128)(2,1)S(1)} collective-permute-done((bf16[2,176,512]{2,1,0:T(8,128)(2,1)S(1)}, bf16[2,176,512]{2,1,0:T(8,128)(2,1)S(1)}, u32[]{:S(2)}, u32[]{:S(2)}) %collective-permute-start.6) | collective-permute-done | bytes 360480 | tf_op jit(solution)/shard_map/ppermute | solution.py:1267
  183.0 2.0 collective-permute-start.12
  187.8 2.3 shard_map.297
  190.1 4.9 %collective-permute-done.12.refs_1_ = bf16[128,512]{1,0:T(8,128)(2,1)S(1)} collective-permute-done((bf16[128,512]{1,0:T(8,128)(2,1)S(1)}, bf16[128,512]{1,0:T(8,128)(2,1)S(1)}, u32[]{:S(2)}, u32[]{:S(2)}) %collective-permute-start.12) | collective-permute-done | bytes 131104 | tf_op jit(solution)/shard_map/ppermute | solution.py:1171
  196.3 2.6 %collective-permute-done.14.refs_3_ = bf16[128,512]{1,0:T(8,128)(2,1)S(1)} collective-permute-done((bf16[128,512]{1,0:T(8,128)(2,1)S(1)}, bf16[128,512]{1,0:T(8,128)(2,1)S(1)}, u32[]{:S(2)}, u32[]{:S(2)}) %collective-permute-start.14) | collective-permute-done | bytes 131104 | tf_op jit(solution)/shard_map/ppermute | solution.py:1171
  199.6 4.4 %all-to-all-start.3 = ((bf16[8,160,512]{2,1,0:T(8,128)(2,1)}), bf16[8,160,512]{2,1,0:T(8,128)(2,1)S(1)}, u32[]{:S(2)}, u32[]{:S(2)}) async-start(bf16[8,160,512]{2,1,0:T(8,128)(2,1)} %shard_map.297), calls=%async_computation.3 | async-start | bytes 2621440 | tf_op jit(solution)/shard_map/all_to_all | solution.py:1309
  209.0 25.6 %all-to-all-done.3.both = bf16[8,160,512]{2,1,0:T(8,128)(2,1)S(1)} async-done(((bf16[8,160,512]{2,1,0:T(8,128)(2,1)}), bf16[8,160,512]{2,1,0:T(8,128)(2,1)S(1)}, u32[]{:S(2)}, u32[]{:S(2)}) %all-to-all-start.3) | async-done | bytes 1310752 | tf_op jit(solution)/shard_map/all_to_all | solution.py:1309
  234.7 1.9 shard_map.298
  238.4 2.9 %collective-permute-done.17.refs_2_ = bf16[64,512]{1,0:T(8,128)(2,1)S(1)} collective-permute-done((bf16[64,512]{1,0:T(8,128)(2,1)}, bf16[64,512]{1,0:T(8,128)(2,1)S(1)}, u32[]{:S(2)}, u32[]{:S(2)}) %collective-permute-start.17) | collective-permute-done | bytes 65568 | tf_op jit(solution)/shard_map/ppermute | solution.py:1336
  242.4 1.8 shard_map.301
  (116 shorter events, 28.5 us)
Async XLA Ops:
  32.1 2.4 collective-permute-start
  35.4 45.6 %copy-start.17 = (bf16[512,512]{1,0:T(8,128)(2,1)S(1)}, bf16[512,512]{1,0:T(8,128)(2,1)}, u32[]{:S(2)}) copy-start(bf16[512,512]{1,0:T(8,128)(2,1)} %wfo_hbm.1) | copy-start | bytes 1572868
  114.0 7.0 %collective-permute-start.1 = (bf16[8,256,512]{2,1,0:T(8,128)(2,1)}, bf16[8,256,512]{2,1,0:T(8,128)(2,1)S(1)}, u32[]{:S(2)}, u32[]{:S(2)}) collective-permute-start(bf16[8,256,512]{2,1,0:T(8,128)(2,1)} %get-tuple-element.96), channel_id=1, source_target_pairs={{0,1},{1,0},{2,3},{3,2},{4,5},{5,4},{6,7},{7,6},{8,9},{9,8},{10,11... | collective-permute-start | bytes 6291464 | tf_op jit(solution)/shard_map/ppermute | solution.py:1161
  114.9 6.1 %collective-permute-start.2 = (bf16[8,176,512]{2,1,0:T(8,128)(2,1)}, bf16[8,176,512]{2,1,0:T(8,128)(2,1)}, u32[]{:S(2)}, u32[]{:S(2)}) collective-permute-start(bf16[8,176,512]{2,1,0:T(8,128)(2,1)} %get-tuple-element.98), channel_id=1, source_target_pairs={{0,1},{1,0},{2,3},{3,2},{4,5},{5,4},{6,7},{7,6},{8,9},{9,8},{10,11... | collective-permute-start | bytes 4325384 | tf_op jit(solution)/shard_map/ppermute | solution.py:1162
  115.0 23.1 %all-to-all-start.2 = ((bf16[16,96,256]{2,1,0:T(8,128)(2,1)}), bf16[16,96,256]{2,1,0:T(8,128)(2,1)}, u32[]{:S(2)}, u32[]{:S(2)}) async-start(bf16[16,96,256]{2,1,0:T(8,128)(2,1)} %copy-done.12), calls=%async_computation.2 | async-start | bytes 1572864 | tf_op jit(solution)/shard_map/all_to_all | solution.py:1163
  128.0 27.6 %collective-permute-start.3 = (bf16[8,128,512]{2,1,0:T(8,128)(2,1)}, bf16[8,128,512]{2,1,0:T(8,128)(2,1)S(1)}, u32[]{:S(2)}, u32[]{:S(2)}) collective-permute-start(bf16[8,128,512]{2,1,0:T(8,128)(2,1)} %get-tuple-element.109), channel_id=1, source_target_pairs={{0,16},{16,0},{1,17},{17,1},{2,18},{18,2},{3,19},{19,3},{4,20},{20... | collective-permute-start | bytes 3145736 | tf_op jit(solution)/shard_map/ppermute | solution.py:985
  129.5 26.1 %collective-permute-start.4 = (bf16[4,176,512]{2,1,0:T(8,128)(2,1)}, bf16[4,176,512]{2,1,0:T(8,128)(2,1)}, u32[]{:S(2)}, u32[]{:S(2)}) collective-permute-start(bf16[4,176,512]{2,1,0:T(8,128)(2,1)} %get-tuple-element.111), channel_id=1, source_target_pairs={{0,2},{1,3},{2,0},{3,1},{4,6},{5,7},{6,4},{7,5},{8,10},{9,11},{10,... | collective-permute-start | bytes 2162696 | tf_op jit(solution)/shard_map/ppermute | solution.py:1188
  161.6 20.5 %collective-permute-start.5 = (bf16[4,128,512]{2,1,0:T(8,128)(2,1)S(1)}, bf16[4,128,512]{2,1,0:T(8,128)(2,1)S(1)}, u32[]{:S(2)}, u32[]{:S(2)}) collective-permute-start(bf16[4,128,512]{2,1,0:T(8,128)(2,1)S(1)} %get-tuple-element.121), channel_id=1, source_target_pairs={{0,2},{1,3},{2,0},{3,1},{4,6},{5,7},{6,4},{7,5},{8,10},{9,11},{10,... | collective-permute-start | bytes 1572872 | tf_op jit(solution)/shard_map/ppermute | solution.py:1266
  162.8 19.3 %collective-permute-start.6 = (bf16[2,176,512]{2,1,0:T(8,128)(2,1)S(1)}, bf16[2,176,512]{2,1,0:T(8,128)(2,1)S(1)}, u32[]{:S(2)}, u32[]{:S(2)}) collective-permute-start(bf16[2,176,512]{2,1,0:T(8,128)(2,1)S(1)} %get-tuple-element.123), channel_id=1, source_target_pairs={{0,8},{1,9},{2,10},{3,11},{4,12},{5,13},{6,14},{7,15},{8,0},{9,1},... | collective-permute-start | bytes 1081352 | tf_op jit(solution)/shard_map/ppermute | solution.py:1267
  165.5 22.3 %collective-permute-start.11 = (bf16[8,64,512]{2,1,0:T(8,128)(2,1)S(1)}, bf16[8,64,512]{2,1,0:T(8,128)(2,1)S(1)}, u32[]{:S(2)}, u32[]{:S(2)}) collective-permute-start(bf16[8,64,512]{2,1,0:T(8,128)(2,1)S(1)} %get-tuple-element.116), channel_id=1, source_target_pairs={{0,16},{16,0},{1,17},{17,1},{2,18},{18,2},{3,19},{19,3},{4,20},{20... | collective-permute-start | bytes 1572872 | tf_op jit(solution)/shard_map/ppermute | solution.py:985
  170.8 12.0 %collective-permute-start.7 = (bf16[2,96,512]{2,1,0:T(8,128)(2,1)S(1)}, bf16[2,96,512]{2,1,0:T(8,128)(2,1)S(1)}, u32[]{:S(2)}, u32[]{:S(2)}) collective-permute-start(bf16[2,96,512]{2,1,0:T(8,128)(2,1)S(1)} %get-tuple-element.129), channel_id=1, source_target_pairs={{0,1},{1,0},{2,3},{3,2},{4,5},{5,4},{6,7},{7,6},{8,9},{9,8},{10,11... | collective-permute-start | bytes 589832 | tf_op jit(solution)/shard_map/ppermute | solution.py:1282
  170.9 12.1 %collective-permute-start.8 = (bf16[2,96,512]{2,1,0:T(8,128)(2,1)S(1)}, bf16[2,96,512]{2,1,0:T(8,128)(2,1)S(1)}, u32[]{:S(2)}, u32[]{:S(2)}) collective-permute-start(bf16[2,96,512]{2,1,0:T(8,128)(2,1)S(1)} %get-tuple-element.130), channel_id=1, source_target_pairs={{0,1},{1,0},{2,3},{3,2},{4,5},{5,4},{6,7},{7,6},{8,9},{9,8},{10,11... | collective-permute-start | bytes 589832 | tf_op jit(solution)/shard_map/ppermute | solution.py:1282
  182.1 2.8 %collective-permute-start.9 = (bf16[2,96,512]{2,1,0:T(8,128)(2,1)S(1)}, bf16[2,96,512]{2,1,0:T(8,128)(2,1)S(1)}, u32[]{:S(2)}, u32[]{:S(2)}) collective-permute-start(bf16[2,96,512]{2,1,0:T(8,128)(2,1)S(1)} %get-tuple-element.131), channel_id=1, source_target_pairs={{0,1},{1,0},{2,3},{3,2},{4,5},{5,4},{6,7},{7,6},{8,9},{9,8},{10,11... | collective-permute-start | bytes 589832 | tf_op jit(solution)/shard_map/ppermute | solution.py:1282
  182.1 4.2 %collective-permute-start.10 = (bf16[2,96,512]{2,1,0:T(8,128)(2,1)S(1)}, bf16[2,96,512]{2,1,0:T(8,128)(2,1)S(1)}, u32[]{:S(2)}, u32[]{:S(2)}) collective-permute-start(bf16[2,96,512]{2,1,0:T(8,128)(2,1)S(1)} %get-tuple-element.132), channel_id=1, source_target_pairs={{0,1},{1,0},{2,3},{3,2},{4,5},{5,4},{6,7},{7,6},{8,9},{9,8},{10,11... | collective-permute-start | bytes 589832 | tf_op jit(solution)/shard_map/ppermute | solution.py:1282
  182.9 16.7 %collective-permute-start.15 = (bf16[176,512]{1,0:T(8,128)(2,1)S(1)}, bf16[176,512]{1,0:T(8,128)(2,1)S(1)}, u32[]{:S(2)}, u32[]{:S(2)}) collective-permute-start(bf16[176,512]{1,0:T(8,128)(2,1)S(1)} %get-tuple-element.138), channel_id=1, source_target_pairs={{0,4},{1,5},{2,6},{3,7},{4,0},{5,1},{6,2},{7,3},{8,12},{9,13},{10,... | collective-permute-start | bytes 540680 | tf_op jit(solution)/shard_map/ppermute | solution.py:1171
  183.0 12.1 %collective-permute-start.12 = (bf16[128,512]{1,0:T(8,128)(2,1)S(1)}, bf16[128,512]{1,0:T(8,128)(2,1)S(1)}, u32[]{:S(2)}, u32[]{:S(2)}) collective-permute-start(bf16[128,512]{1,0:T(8,128)(2,1)S(1)} %get-tuple-element.134), channel_id=1, source_target_pairs={{0,4},{1,5},{2,6},{3,7},{4,0},{5,1},{6,2},{7,3},{8,12},{9,13},{10,... | collective-permute-start | bytes 393224 | tf_op jit(solution)/shard_map/ppermute | solution.py:1171
  185.0 10.7 %collective-permute-start.13 = (bf16[128,512]{1,0:T(8,128)(2,1)S(1)}, bf16[128,512]{1,0:T(8,128)(2,1)S(1)}, u32[]{:S(2)}, u32[]{:S(2)}) collective-permute-start(bf16[128,512]{1,0:T(8,128)(2,1)S(1)} %get-tuple-element.135), channel_id=1, source_target_pairs={{0,8},{1,9},{2,10},{3,11},{4,12},{5,13},{6,14},{7,15},{8,0},{9,1},... | collective-permute-start | bytes 393224 | tf_op jit(solution)/shard_map/ppermute | solution.py:1171
  186.3 12.6 %collective-permute-start.14 = (bf16[128,512]{1,0:T(8,128)(2,1)S(1)}, bf16[128,512]{1,0:T(8,128)(2,1)S(1)}, u32[]{:S(2)}, u32[]{:S(2)}) collective-permute-start(bf16[128,512]{1,0:T(8,128)(2,1)S(1)} %get-tuple-element.136), channel_id=1, source_target_pairs={{0,12},{1,13},{2,14},{3,15},{4,8},{5,9},{6,10},{7,11},{8,4},{9,5},... | collective-permute-start | bytes 393224 | tf_op jit(solution)/shard_map/ppermute | solution.py:1171
  199.6 35.1 %all-to-all-start.3 = ((bf16[8,160,512]{2,1,0:T(8,128)(2,1)}), bf16[8,160,512]{2,1,0:T(8,128)(2,1)S(1)}, u32[]{:S(2)}, u32[]{:S(2)}) async-start(bf16[8,160,512]{2,1,0:T(8,128)(2,1)} %shard_map.297), calls=%async_computation.3 | async-start | bytes 2621440 | tf_op jit(solution)/shard_map/all_to_all | solution.py:1309
  204.1 34.4 %collective-permute-start.20 = (bf16[176,512]{1,0:T(8,128)(2,1)S(1)}, bf16[176,512]{1,0:T(8,128)(2,1)S(1)}, u32[]{:S(2)}, u32[]{:S(2)}) collective-permute-start(bf16[176,512]{1,0:T(8,128)(2,1)S(1)} %shard_map.300.refs_6_), channel_id=1, source_target_pairs={{0,16},{16,0},{1,17},{17,1},{2,18},{18,2},{3,19},{19,3},{4,20},{20... | collective-permute-start | bytes 540680 | tf_op jit(solution)/shard_map/ppermute | solution.py:985
  208.4 30.0 %collective-permute-start.19 = (bf16[128,512]{1,0:T(8,128)(2,1)S(1)}, bf16[128,512]{1,0:T(8,128)(2,1)S(1)}, u32[]{:S(2)}, u32[]{:S(2)}) collective-permute-start(bf16[128,512]{1,0:T(8,128)(2,1)S(1)} %shard_map.299.refs_4_), channel_id=1, source_target_pairs={{0,16},{16,0},{1,17},{17,1},{2,18},{18,2},{3,19},{19,3},{4,20},{20... | collective-permute-start | bytes 393224 | tf_op jit(solution)/shard_map/ppermute | solution.py:985
  236.6 1.9 collective-permute-start.16
  236.6 4.8 %collective-permute-start.17 = (bf16[64,512]{1,0:T(8,128)(2,1)}, bf16[64,512]{1,0:T(8,128)(2,1)S(1)}, u32[]{:S(2)}, u32[]{:S(2)}) collective-permute-start(bf16[64,512]{1,0:T(8,128)(2,1)} %get-tuple-element.141.refs_0_), channel_id=1, source_target_pairs={{0,16},{1,17},{2,18},{3,19},{4,20},{5,21},{6,22},{7,23},{8,24},{9,... | collective-permute-start | bytes 196616 | tf_op jit(solution)/shard_map/ppermute | solution.py:1336
  238.1 4.3 %collective-permute-start.18 = (bf16[64,512]{1,0:T(8,128)(2,1)}, bf16[64,512]{1,0:T(8,128)(2,1)S(1)}, u32[]{:S(2)}, u32[]{:S(2)}) collective-permute-start(bf16[64,512]{1,0:T(8,128)(2,1)} %get-tuple-element.141.refs_0_), channel_id=1, source_target_pairs={{0,17},{1,16},{2,19},{3,18},{4,21},{5,20},{6,23},{7,22},{8,25},{9,... | collective-permute-start | bytes 196616 | tf_op jit(solution)/shard_map/ppermute | solution.py:1336
  (34 other events, 401.8 us)
